TPU v7x, 32 devices: a whole 2x2x4 slice. The times are simulated.
32 devices in a mesh: tm: 4 (over y, core), height: 4 (over z), dp: 2 (over x).
Axes of the slice: x: 2, y: 2, z: 4, core: 2. Of those that a mesh axis runs over, the one named last changes fastest.
Arguments:
- queries: bfloat16 [4, 4, 4, 1, 192, 128], P('tm', 'height', 'dp'), may hold values from -4.5 to 4.5
- keys: bfloat16 [4, 4, 4, 1, 192, 128], P('tm', 'height', 'dp'), may hold values from -4.5 to 4.5
- values: bfloat16 [4, 4, 4, 1, 192, 128], P('tm', 'height', 'dp'), may hold values from -6 to 6
- grad_out: bfloat16 [4, 4, 4, 1, 192, 128], P('tm', 'height', 'dp'), may hold values from -24 to 24
- attn_out: bfloat16 [4, 4, 4, 1, 192, 128], P('tm', 'height', 'dp'), may hold values from -1.796875 to 1.796875
- window_mask: int32 [4, 4, 1, 27], P('tm', 'height'), may hold values 0 or 1
Outputs:
- grad_queries: bfloat16 [4, 4, 4, 1, 192, 128], P('tm', 'height', 'dp')
- grad_keys: bfloat16 [4, 4, 4, 1, 192, 128], P('tm', 'height', 'dp')
- grad_values: bfloat16 [4, 4, 4, 1, 192, 128], P('tm', 'height', 'dp')
All inputs are finite; a program needn't handle non-finite values. No bound on the sum of `window_mask` on one device may be relied on, other than what follows from the above.
Results may differ from a plain program's by a relative error of at most 0.009.
Values may be sent and summed in bfloat16 or wider, within the bound.
No kernel may reach another device: no remote copies, remote signals or barrier semaphores. Data moves between devices by JAX's collectives and lax.ppermute only.
A program may use at most 64 MiB of HBM per device.

v0:
```python
import functools

import jax
import jax.numpy as jnp
from jax import lax
from jax.experimental import pallas as pl
from jax.experimental.pallas import tpu as pltpu
from jax.sharding import PartitionSpec as P

VMEM = pl.BlockSpec(memory_space=pltpu.VMEM)
HBM = pl.BlockSpec(memory_space=pltpu.HBM)
LIMIT = pltpu.CompilerParams(vmem_limit_bytes=32 * 1024 * 1024)
ROWS_T = (((1,), (1,)), ((), ()))
COLS_T = (((0,), (0,)), ((), ()))


def dot(a, b, dims=(((1,), (0,)), ((), ()))):
    return lax.dot_general(a, b, dims, preferred_element_type=jnp.float32)


def place():
    t = lax.axis_index("tm")
    return t // 2, t % 2, lax.axis_index("height")


def pair(index, which):
    rising = (index % 2) == (0 if which == 0 else 1)
    return rising, jnp.where(rising, index + 1, index - 1)


def within(index, size):
    return (index >= 0) & (index < size)


def tile_rows(index, tok):
    return pl.ds(pl.multiple_of(index * tok, tok), tok)


def pack_kernel(tok, k_ref, v_ref, q_ref, g_ref, o_ref, mask_ref, own_ref, other_ref, flags, sems):
    _, c, _ = place()
    copies = [pltpu.make_async_copy(mask_ref, flags, sems.at[10])]
    for i, ref in enumerate((k_ref, v_ref, q_ref, g_ref, o_ref)):
        rows = pl.ds(i * tok, tok)
        copies.append(pltpu.make_async_copy(ref.at[0, 0, 1 - c, 0], other_ref.at[rows, :], sems.at[2 * i]))
        copies.append(pltpu.make_async_copy(ref.at[0, 0, c, 0], own_ref.at[rows, :], sems.at[2 * i + 1]))
    for copy in copies:
        copy.start()
    copies[0].wait()
    row = lax.broadcasted_iota(jnp.int32, (16, own_ref.shape[1]), 0)
    spread = jnp.zeros(row.shape, jnp.float32)
    for i in range(9):
        on = (flags[0, 0, 0, 9 * (i // 3) + 3 * (i % 3) + 1] != 0).astype(jnp.float32)
        spread = jnp.where(row == i, on, spread)
    own_ref[pl.ds(5 * tok, 16), :] = spread.astype(jnp.bfloat16)
    other_ref[pl.ds(5 * tok, 16), :] = spread.astype(jnp.bfloat16)
    for copy in copies[1:]:
        copy.wait()


def line_kernel(tok, own_ref, par_ref, line_ref, *border_refs):
    y, c, _ = place()
    for i in range(2):
        rows = pl.ds(i * tok, tok)
        line_ref[i, tile_rows(c, tok), :] = own_ref[rows, :]
        line_ref[i, tile_rows(1 - c, tok), :] = par_ref[rows, :]
        for which, ref in enumerate(border_refs):
            rising, _ = pair(y, which)
            ref[i] = jnp.where((c == 1) == rising, own_ref[rows, :], par_ref[rows, :])


def main_kernel(tok, chips, heights, sides, scale, *refs):
    own_ref, par_ref = refs[:2]
    count = 3 * (1 + sides)
    sources, results = refs[2 : 2 + count], refs[2 + count : 2 + 2 * count]
    dq_ref, qs, gs, s_ref = refs[2 + 2 * count :]
    y, c, z = place()
    two = 2 * tok
    width = own_ref.shape[1]
    f32, bf16 = jnp.float32, jnp.bfloat16
    first = c == 0

    def by_tile(part):
        own, par = own_ref[pl.ds(part * tok, tok), :], par_ref[pl.ds(part * tok, tok), :]
        return own, par

    for part, ref in ((2, qs), (3, gs)):
        own, par = by_tile(part)
        ref[tile_rows(c, tok), :] = own
        ref[tile_rows(1 - c, tok), :] = par
    (g_own, g_par), (o_own, o_par) = by_tile(3), by_tile(4)
    p_own, p_par = g_own.astype(f32) * o_own.astype(f32), g_par.astype(f32) * o_par.astype(f32)
    product = jnp.concatenate([jnp.where(first, p_own, p_par), jnp.where(first, p_par, p_own)], axis=0)
    delta = jnp.sum(product.T, axis=0, keepdims=True)

    lane = lax.broadcasted_iota(jnp.int32, (1, width), 1)
    own_flags = own_ref[pl.ds(5 * tok, 16), :].astype(f32)
    par_flags = par_ref[pl.ds(5 * tok, 16), :].astype(f32)
    flags = jnp.where(first, own_flags, par_flags), jnp.where(first, par_flags, own_flags)
    none = jnp.zeros((1, width), f32)

    def bias(line, slot):
        inside = True
        if line:
            z_rising, z_at = pair(z, line - 1)
            inside = within(z_at, heights)

        def at(tile, dt):
            row = flags[tile]
            if line == 0:
                return row[3 * dt + 1 : 3 * dt + 2] if dt != 1 else none + 1.0
            return jnp.where(z_rising, row[3 * dt + 2 : 3 * dt + 3], row[3 * dt : 3 * dt + 1])

        if slot == 0:
            even, odd = at(0, 1), at(1, 0)
        elif slot == 1:
            even, odd = at(0, 2), at(1, 1)
        else:
            y_rising, y_at = pair(y, slot - 2)
            inside = within(y_at, chips) & inside
            even, odd = jnp.where(y_rising, none, at(0, 0)), jnp.where(y_rising, at(1, 2), none)
        row = jnp.concatenate([jnp.where(lane + start < tok, even, odd) for start in range(0, two, width)], axis=1)
        return jnp.where(inside, (row - 1.0) * 1e30, -1e30)

    blocks = []
    for line in range(3):
        for slot in range(2 + sides):
            at = line * (1 + sides) + max(slot - 1, 0)
            blocks.append((line, slot, at, pl.ds(tok if slot == 1 else 0, tok), pl.ds(len(blocks) * tok, tok)))

    top = jnp.full((8, two), -1e30, f32)
    for line, slot, at, rows, kept in blocks:
        scores = dot(sources[at][0, rows, :], qs[...], ROWS_T) * scale + bias(line, slot)
        s_ref[kept, :] = scores
        top = jnp.maximum(top, jnp.max(scores.reshape(tok // 8, 8, two), axis=0))
    top = jnp.max(top, axis=0, keepdims=True)
    total = jnp.zeros((8, two), f32)
    for _, _, _, _, kept in blocks:
        weights = jnp.exp(s_ref[kept, :] - top)
        s_ref[kept, :] = weights
        total = total + jnp.sum(weights.reshape(tok // 8, 8, two), axis=0)
    share = 1.0 / jnp.sum(total, axis=0, keepdims=True)

    dq = jnp.zeros((two, width), f32)
    for _, _, at, rows, kept in blocks:
        probs = s_ref[kept, :] * share
        grads = dot(sources[at][1, rows, :], gs[...], ROWS_T)
        low = (probs * (grads - delta) * scale).astype(bf16)
        results[at][0, rows, :] = dot(low, qs[...]).astype(bf16)
        results[at][1, rows, :] = dot(probs.astype(bf16), gs[...]).astype(bf16)
        dq = dq + dot(low, sources[at][0, rows, :], COLS_T)
    dq_ref[...] = dq.astype(bf16)


def sum_kernel(tok, chips, heights, sides, *refs):
    count = 3 * (1 + sides)
    parts, (dq_ref, mine_ref, swap_ref) = refs[:count], refs[count:]
    y, c, z = place()

    def total(i, tile):
        value = jnp.zeros(mine_ref.shape[1:], jnp.float32)
        for line in range(3):
            inside = True
            if line:
                _, z_at = pair(z, line - 1)
                inside = within(z_at, heights)
            block = parts[line * (1 + sides)][i, tile_rows(tile, tok), :].astype(jnp.float32)
            value = value + (jnp.where(inside, block, 0.0) if line else block)
            for which in range(sides):
                y_rising, y_at = pair(y, which)
                halo = parts[line * (1 + sides) + 1 + which][i].astype(jnp.float32)
                value = value + jnp.where(((tile == 1) == y_rising) & within(y_at, chips) & inside, halo, 0.0)
        return value

    for i in range(2):
        mine_ref[i] = total(i, c)
        swap_ref[i] = total(i, 1 - c).astype(jnp.bfloat16)
    swap_ref[2] = dq_ref[tile_rows(1 - c, tok), :]


def final_kernel(tok, mine_ref, swap_ref, dq_ref, gq_ref, gk_ref, gv_ref):
    _, c, _ = place()
    gq_ref[0, 0, c, 0] = dq_ref[tile_rows(c, tok), :]
    gq_ref[0, 0, 1 - c, 0] = swap_ref[2]
    for i, ref in enumerate((gk_ref, gv_ref)):
        ref[0, 0, c, 0] = mine_ref[i].astype(jnp.bfloat16)
        ref[0, 0, 1 - c, 0] = swap_ref[i]


def body(queries, keys, values, grad_out, attn_out, window_mask):
    tok, width = queries.shape[-2:]
    scale = width ** -0.5
    times, heights = lax.axis_size("tm"), lax.axis_size("height")
    chips = times // 2
    sides = 1 if chips == 2 else 2
    bf16, f32 = jnp.bfloat16, jnp.float32

    def call(kernel, shapes, specs, scratch=()):
        return pl.pallas_call(
            kernel,
            out_shape=[jax.ShapeDtypeStruct(*shape) for shape in shapes],
            in_specs=list(specs),
            out_specs=[VMEM] * len(shapes),
            scratch_shapes=list(scratch),
            compiler_params=LIMIT,
        )

    def partner(index, which, size):
        if which is None:
            return index
        at = index + 1 if index % 2 == which else index - 1
        return at if 0 <= at < size else None

    def exchange(block, y_which, z_which):
        pairs = []
        for t in range(times):
            for z in range(heights):
                y_at, z_at = partner(t // 2, y_which, chips), partner(z, z_which, heights)
                at = t * heights + z
                alone = y_at is None or z_at is None
                pairs.append((at, (t ^ 1) * heights + z if alone else (2 * y_at + t % 2) * heights + z_at))
        return lax.ppermute(block, ("tm", "height"), pairs)

    def swap_cores(block):
        return lax.ppermute(block, "tm", [(t, t ^ 1) for t in range(times)])

    def exchange_all(lines, halos):
        found = {(j, 0): exchange(lines[j], None, j - 1) for j in (1, 2)}
        for j in range(3):
            for which in range(sides):
                found[j, 1 + which] = exchange(halos[j][which], which, None if j == 0 else j - 1)
        return found

    packed = ((5 * tok + 16, width), bf16)
    arguments = (keys, values, queries, grad_out, attn_out, window_mask)
    own, other = call(
        functools.partial(pack_kernel, tok),
        [packed, packed],
        [HBM] * 6,
        [pltpu.SMEM(window_mask.shape, jnp.int32), pltpu.SemaphoreType.DMA((11,))],
    )(*(pltpu.with_memory_space_constraint(x, pltpu.HBM) for x in arguments))
    par = swap_cores(other)
    line_shape, tile_shape = ((2, 2 * tok, width), bf16), ((2, tok, width), bf16)
    line, *borders = call(
        functools.partial(line_kernel, tok), [line_shape] + [tile_shape] * sides, [VMEM] * 2
    )(own, par)
    found = exchange_all([None, line, line], [borders] * 3)
    found[0, 0] = line
    order = [(j, k) for j in range(3) for k in range(1 + sides)]
    *columns, dq = call(
        functools.partial(main_kernel, tok, chips, heights, sides, scale),
        [line_shape if k == 0 else tile_shape for _, k in order] + [((2 * tok, width), bf16)],
        [VMEM] * (2 + len(order)),
        [
            pltpu.VMEM((2 * tok, width), bf16),
            pltpu.VMEM((2 * tok, width), bf16),
            pltpu.VMEM((3 * (2 + sides) * tok, 2 * tok), f32),
        ],
    )(own, par, *(found[at] for at in order))
    columns = dict(zip(order, columns))
    back = exchange_all(
        [columns[j, 0] for j in range(3)], [[columns[j, 1 + k] for k in range(sides)] for j in range(3)]
    )
    back[0, 0] = columns[0, 0]
    mine, leaving = call(
        functools.partial(sum_kernel, tok, chips, heights, sides),
        [((2, tok, width), f32), ((3, tok, width), bf16)],
        [VMEM] * (len(order) + 1),
    )(*(back[at] for at in order), dq)
    return call(
        functools.partial(final_kernel, tok),
        [(queries.shape, bf16)] * 3,
        [VMEM] * 3,
    )(mine, swap_cores(leaving), dq)


def solution(mesh):
    placed = P("tm", "height", "dp", None, None, None)
    return jax.shard_map(
        body,
        mesh=mesh,
        in_specs=(placed,) * 5 + (P("tm", "height", None, None),),
        out_specs=(placed,) * 3,
        check_vma=False,
    )
```

profile of v0, /device:TPU:0, one launch (start us, length us, event | category | flops | bytes accessed | tf_op | source)
XLA Modules:
  0.0 33.1 jit_solution(11898143010883112600)
XLA Ops:
  0.6 1.1 %shard_map.85 = (bf16[976,128]{1,0:T(8,128)(2,1)S(1)}, bf16[976,128]{1,0:T(8,128)(2,1)S(1)}) custom-call(bf16[1,1,2,1,192,128]{5,4,3,2,1,0:T(8,128)(2,1)} %k_ref.1, bf16[1,1,2,1,192,128]{5,4,3,2,1,0:T(8,128)(2,1)} %v_ref.1, bf16[1,1,2,1,192,128]{5,4,3,2,1,0:T(8,128)(2,1)} %q_ref.1, bf16[1,1,2,1,192,128]{5,4,3,2,1,0:T(8,128)(2,1)} %g_ref.1, ...), custom_call_target="tpu_custom_call" | custom-call | tf_op jit(solution)/shard_map/pallas_call | solution.py:235
  1.8 0.5 %collective-permute-start = (bf16[976,128]{1,0:T(8,128)(2,1)S(1)}, bf16[976,128]{1,0:T(8,128)(2,1)S(1)}, u32[]{:S(2)}, u32[]{:S(2)}) collective-permute-start(bf16[976,128]{1,0:T(8,128)(2,1)S(1)} %get-tuple-element.17), channel_id=1, source_target_pairs={{0,8},{8,0},{16,24},{24,16},{1,9},{9,1},{17,25},{25,17},{2,10},{10... | collective-permute-start | bytes 749576 | tf_op jit(solution)/shard_map/ppermute | solution.py:224
  2.3 1.1 %collective-permute-done.par_ref.refs_1_ = bf16[976,128]{1,0:T(8,128)(2,1)S(1)} collective-permute-done((bf16[976,128]{1,0:T(8,128)(2,1)S(1)}, bf16[976,128]{1,0:T(8,128)(2,1)S(1)}, u32[]{:S(2)}, u32[]{:S(2)}) %collective-permute-start) | collective-permute-done | bytes 249888 | tf_op jit(solution)/shard_map/ppermute | solution.py:224
  3.4 0.1 shard_map.86
  3.5 0.4 %collective-permute-start.4 = (bf16[2,384,128]{2,1,0:T(8,128)(2,1)S(1)}, bf16[2,384,128]{2,1,0:T(8,128)(2,1)S(1)}, u32[]{:S(2)}, u32[]{:S(2)}) collective-permute-start(bf16[2,384,128]{2,1,0:T(8,128)(2,1)S(1)} %get-tuple-element.18.refs_2_), channel_id=1, source_target_pairs={{0,8},{2,4},{4,2},{6,14},{8,0},{10,12},{12,10},{14,6},{16,24},{18,... | collective-permute-start | bytes 589832 | tf_op jit(solution)/shard_map/ppermute | solution.py:221
  3.9 4.1 %collective-permute-start.2 = (bf16[2,384,128]{2,1,0:T(8,128)(2,1)S(1)}, bf16[2,384,128]{2,1,0:T(8,128)(2,1)S(1)}, u32[]{:S(2)}, u32[]{:S(2)}) collective-permute-start(bf16[2,384,128]{2,1,0:T(8,128)(2,1)S(1)} %get-tuple-element.18.refs_2_), channel_id=1, source_target_pairs={{0,2},{2,0},{4,6},{6,4},{8,10},{10,8},{12,14},{14,12},{16,18},{18,... | collective-permute-start | bytes 589832 | tf_op jit(solution)/shard_map/ppermute | solution.py:221
  8.1 2.6 %collective-permute-start.3 = (bf16[2,192,128]{2,1,0:T(8,128)(2,1)S(1)}, bf16[2,192,128]{2,1,0:T(8,128)(2,1)S(1)}, u32[]{:S(2)}, u32[]{:S(2)}) collective-permute-start(bf16[2,192,128]{2,1,0:T(8,128)(2,1)S(1)} %get-tuple-element.19), channel_id=1, source_target_pairs={{0,18},{2,16},{4,22},{6,20},{8,26},{10,24},{12,30},{14,28},{16,2},... | collective-permute-start | bytes 294920 | tf_op jit(solution)/shard_map/ppermute | solution.py:221
  10.7 1.5 %collective-permute-start.1 = (bf16[2,192,128]{2,1,0:T(8,128)(2,1)S(1)}, bf16[2,192,128]{2,1,0:T(8,128)(2,1)S(1)}, u32[]{:S(2)}, u32[]{:S(2)}) collective-permute-start(bf16[2,192,128]{2,1,0:T(8,128)(2,1)S(1)} %get-tuple-element.19), channel_id=1, source_target_pairs={{0,16},{2,18},{4,20},{6,22},{8,24},{10,26},{12,28},{14,30},{16,0},... | collective-permute-start | bytes 294920 | tf_op jit(solution)/shard_map/ppermute | solution.py:221
  12.2 0.0 collective-permute-done.5.refs_7_
  12.2 3.9 %collective-permute-done.3.refs_5_ = bf16[2,192,128]{2,1,0:T(8,128)(2,1)S(1)} collective-permute-done((bf16[2,192,128]{2,1,0:T(8,128)(2,1)S(1)}, bf16[2,192,128]{2,1,0:T(8,128)(2,1)S(1)}, u32[]{:S(2)}, u32[]{:S(2)}) %collective-permute-start.3) | collective-permute-done | bytes 98336 | tf_op jit(solution)/shard_map/ppermute | solution.py:221
  16.2 0.9 %collective-permute-done.1.refs_3_ = bf16[2,192,128]{2,1,0:T(8,128)(2,1)S(1)} collective-permute-done((bf16[2,192,128]{2,1,0:T(8,128)(2,1)S(1)}, bf16[2,192,128]{2,1,0:T(8,128)(2,1)S(1)}, u32[]{:S(2)}, u32[]{:S(2)}) %collective-permute-start.1) | collective-permute-done | bytes 98336 | tf_op jit(solution)/shard_map/ppermute | solution.py:221
  17.0 0.0 collective-permute-done.4.refs_6_
  17.0 0.0 collective-permute-done.2.refs_4_
  17.0 3.2 %shard_map.87 = (bf16[2,384,128]{2,1,0:T(8,128)(2,1)S(1)}, bf16[2,192,128]{2,1,0:T(8,128)(2,1)S(1)}, bf16[2,384,128]{2,1,0:T(8,128)(2,1)S(1)}, bf16[2,192,128]{2...) custom-call(bf16[976,128]{1,0:T(8,128)(2,1)S(1)} %get-tuple-element., ...), custom_call_target="tpu_custom_call" | custom-call | tf_op jit(solution)/shard_map/pallas_call | solution.py:249
  20.2 3.1 %collective-permute-start.7 = (bf16[2,384,128]{2,1,0:T(8,128)(2,1)S(1)}, bf16[2,384,128]{2,1,0:T(8,128)(2,1)S(1)}, u32[]{:S(2)}, u32[]{:S(2)}) collective-permute-start(bf16[2,384,128]{2,1,0:T(8,128)(2,1)S(1)} %get-tuple-element.22), channel_id=1, source_target_pairs={{0,2},{2,0},{4,6},{6,4},{8,10},{10,8},{12,14},{14,12},{16,18},{18,... | collective-permute-start | bytes 589832 | tf_op jit(solution)/shard_map/ppermute | solution.py:221
  23.3 0.0 collective-permute-start.9
  23.3 0.5 %collective-permute-start.6 = (bf16[2,192,128]{2,1,0:T(8,128)(2,1)S(1)}, bf16[2,192,128]{2,1,0:T(8,128)(2,1)S(1)}, u32[]{:S(2)}, u32[]{:S(2)}) collective-permute-start(bf16[2,192,128]{2,1,0:T(8,128)(2,1)S(1)} %get-tuple-element.21), channel_id=1, source_target_pairs={{0,16},{2,18},{4,20},{6,22},{8,24},{10,26},{12,28},{14,30},{16,0},... | collective-permute-start | bytes 294920 | tf_op jit(solution)/shard_map/ppermute | solution.py:221
  23.8 1.6 %collective-permute-start.8 = (bf16[2,192,128]{2,1,0:T(8,128)(2,1)S(1)}, bf16[2,192,128]{2,1,0:T(8,128)(2,1)S(1)}, u32[]{:S(2)}, u32[]{:S(2)}) collective-permute-start(bf16[2,192,128]{2,1,0:T(8,128)(2,1)S(1)} %get-tuple-element.23), channel_id=1, source_target_pairs={{0,18},{2,16},{4,22},{6,20},{8,26},{10,24},{12,30},{14,28},{16,2},... | collective-permute-start | bytes 294920 | tf_op jit(solution)/shard_map/ppermute | solution.py:221
  25.4 0.0 collective-permute-start.10
  25.4 5.2 %collective-permute-done.6.refs_1_ = bf16[2,192,128]{2,1,0:T(8,128)(2,1)S(1)} collective-permute-done((bf16[2,192,128]{2,1,0:T(8,128)(2,1)S(1)}, bf16[2,192,128]{2,1,0:T(8,128)(2,1)S(1)}, u32[]{:S(2)}, u32[]{:S(2)}) %collective-permute-start.6) | collective-permute-done | bytes 98336 | tf_op jit(solution)/shard_map/ppermute | solution.py:221
  30.6 0.2 shard_map.88
  30.9 0.1 collective-permute-start.11
  31.0 1.4 %collective-permute-done.11.swap_ref = bf16[3,192,128]{2,1,0:T(8,128)(2,1)S(1)} collective-permute-done((bf16[3,192,128]{2,1,0:T(8,128)(2,1)S(1)}, bf16[3,192,128]{2,1,0:T(8,128)(2,1)S(1)}, u32[]{:S(2)}, u32[]{:S(2)}) %collective-permute-start.11) | collective-permute-done | bytes 147488 | tf_op jit(solution)/shard_map/ppermute | solution.py:224
  32.3 0.7 %shard_map.89 = (bf16[1,1,2,1,192,128]{5,4,3,2,1,0:T(8,128)(2,1)}, bf16[1,1,2,1,192,128]{5,4,3,2,1,0:T(8,128)(2,1)}, bf16[1,1,2,1,192,128]{5,4,3,2,1,0:T(8,128)(2,1)}) custom-call(f32[2,192,128]{2,1,0:T(8,128)S(1)} %get-tuple-element.27.mine_ref, bf16[3,192,128]{2,1,0:T(8,128)(2,1)S(1)} %collective-permute-done.11.swap_ref, ...), custom_call_target="tpu_custom_call" | custom-call | tf_op jit(solution)/shard_map/pallas_call | solution.py:269
  (5 shorter events, 0.0 us)
Async XLA Ops:
  1.8 1.7 %collective-permute-start = (bf16[976,128]{1,0:T(8,128)(2,1)S(1)}, bf16[976,128]{1,0:T(8,128)(2,1)S(1)}, u32[]{:S(2)}, u32[]{:S(2)}) collective-permute-start(bf16[976,128]{1,0:T(8,128)(2,1)S(1)} %get-tuple-element.17), channel_id=1, source_target_pairs={{0,8},{8,0},{16,24},{24,16},{1,9},{9,1},{17,25},{25,17},{2,10},{10... | collective-permute-start | bytes 749576 | tf_op jit(solution)/shard_map/ppermute | solution.py:224
  3.5 13.5 %collective-permute-start.4 = (bf16[2,384,128]{2,1,0:T(8,128)(2,1)S(1)}, bf16[2,384,128]{2,1,0:T(8,128)(2,1)S(1)}, u32[]{:S(2)}, u32[]{:S(2)}) collective-permute-start(bf16[2,384,128]{2,1,0:T(8,128)(2,1)S(1)} %get-tuple-element.18.refs_2_), channel_id=1, source_target_pairs={{0,8},{2,4},{4,2},{6,14},{8,0},{10,12},{12,10},{14,6},{16,24},{18,... | collective-permute-start | bytes 589832 | tf_op jit(solution)/shard_map/ppermute | solution.py:221
  3.9 13.1 %collective-permute-start.2 = (bf16[2,384,128]{2,1,0:T(8,128)(2,1)S(1)}, bf16[2,384,128]{2,1,0:T(8,128)(2,1)S(1)}, u32[]{:S(2)}, u32[]{:S(2)}) collective-permute-start(bf16[2,384,128]{2,1,0:T(8,128)(2,1)S(1)} %get-tuple-element.18.refs_2_), channel_id=1, source_target_pairs={{0,2},{2,0},{4,6},{6,4},{8,10},{10,8},{12,14},{14,12},{16,18},{18,... | collective-permute-start | bytes 589832 | tf_op jit(solution)/shard_map/ppermute | solution.py:221
  8.1 4.1 %collective-permute-start.5 = (bf16[2,192,128]{2,1,0:T(8,128)(2,1)S(1)}, bf16[2,192,128]{2,1,0:T(8,128)(2,1)S(1)}, u32[]{:S(2)}, u32[]{:S(2)}) collective-permute-start(bf16[2,192,128]{2,1,0:T(8,128)(2,1)S(1)} %get-tuple-element.19), channel_id=1, source_target_pairs={{0,8},{2,20},{4,18},{6,14},{8,0},{10,28},{12,26},{14,6},{16,24},{1... | collective-permute-start | bytes 294920 | tf_op jit(solution)/shard_map/ppermute | solution.py:221
  8.1 8.1 %collective-permute-start.3 = (bf16[2,192,128]{2,1,0:T(8,128)(2,1)S(1)}, bf16[2,192,128]{2,1,0:T(8,128)(2,1)S(1)}, u32[]{:S(2)}, u32[]{:S(2)}) collective-permute-start(bf16[2,192,128]{2,1,0:T(8,128)(2,1)S(1)} %get-tuple-element.19), channel_id=1, source_target_pairs={{0,18},{2,16},{4,22},{6,20},{8,26},{10,24},{12,30},{14,28},{16,2},... | collective-permute-start | bytes 294920 | tf_op jit(solution)/shard_map/ppermute | solution.py:221
  10.7 6.3 %collective-permute-start.1 = (bf16[2,192,128]{2,1,0:T(8,128)(2,1)S(1)}, bf16[2,192,128]{2,1,0:T(8,128)(2,1)S(1)}, u32[]{:S(2)}, u32[]{:S(2)}) collective-permute-start(bf16[2,192,128]{2,1,0:T(8,128)(2,1)S(1)} %get-tuple-element.19), channel_id=1, source_target_pairs={{0,16},{2,18},{4,20},{6,22},{8,24},{10,26},{12,28},{14,30},{16,0},... | collective-permute-start | bytes 294920 | tf_op jit(solution)/shard_map/ppermute | solution.py:221
  20.2 10.4 %collective-permute-start.7 = (bf16[2,384,128]{2,1,0:T(8,128)(2,1)S(1)}, bf16[2,384,128]{2,1,0:T(8,128)(2,1)S(1)}, u32[]{:S(2)}, u32[]{:S(2)}) collective-permute-start(bf16[2,384,128]{2,1,0:T(8,128)(2,1)S(1)} %get-tuple-element.22), channel_id=1, source_target_pairs={{0,2},{2,0},{4,6},{6,4},{8,10},{10,8},{12,14},{14,12},{16,18},{18,... | collective-permute-start | bytes 589832 | tf_op jit(solution)/shard_map/ppermute | solution.py:221
  23.3 7.3 %collective-permute-start.9 = (bf16[2,384,128]{2,1,0:T(8,128)(2,1)S(1)}, bf16[2,384,128]{2,1,0:T(8,128)(2,1)S(1)}, u32[]{:S(2)}, u32[]{:S(2)}) collective-permute-start(bf16[2,384,128]{2,1,0:T(8,128)(2,1)S(1)} %get-tuple-element.24), channel_id=1, source_target_pairs={{0,8},{2,4},{4,2},{6,14},{8,0},{10,12},{12,10},{14,6},{16,24},{18,... | collective-permute-start | bytes 589832 | tf_op jit(solution)/shard_map/ppermute | solution.py:221
  23.3 7.3 %collective-permute-start.6 = (bf16[2,192,128]{2,1,0:T(8,128)(2,1)S(1)}, bf16[2,192,128]{2,1,0:T(8,128)(2,1)S(1)}, u32[]{:S(2)}, u32[]{:S(2)}) collective-permute-start(bf16[2,192,128]{2,1,0:T(8,128)(2,1)S(1)} %get-tuple-element.21), channel_id=1, source_target_pairs={{0,16},{2,18},{4,20},{6,22},{8,24},{10,26},{12,28},{14,30},{16,0},... | collective-permute-start | bytes 294920 | tf_op jit(solution)/shard_map/ppermute | solution.py:221
  23.8 6.8 %collective-permute-start.8 = (bf16[2,192,128]{2,1,0:T(8,128)(2,1)S(1)}, bf16[2,192,128]{2,1,0:T(8,128)(2,1)S(1)}, u32[]{:S(2)}, u32[]{:S(2)}) collective-permute-start(bf16[2,192,128]{2,1,0:T(8,128)(2,1)S(1)} %get-tuple-element.23), channel_id=1, source_target_pairs={{0,18},{2,16},{4,22},{6,20},{8,26},{10,24},{12,30},{14,28},{16,2},... | collective-permute-start | bytes 294920 | tf_op jit(solution)/shard_map/ppermute | solution.py:221
  25.4 5.2 %collective-permute-start.10 = (bf16[2,192,128]{2,1,0:T(8,128)(2,1)S(1)}, bf16[2,192,128]{2,1,0:T(8,128)(2,1)S(1)}, u32[]{:S(2)}, u32[]{:S(2)}) collective-permute-start(bf16[2,192,128]{2,1,0:T(8,128)(2,1)S(1)} %get-tuple-element.25), channel_id=1, source_target_pairs={{0,8},{2,20},{4,18},{6,14},{8,0},{10,28},{12,26},{14,6},{16,24},{1... | collective-permute-start | bytes 294920 | tf_op jit(solution)/shard_map/ppermute | solution.py:221
  30.9 1.4 %collective-permute-start.11 = (bf16[3,192,128]{2,1,0:T(8,128)(2,1)S(1)}, bf16[3,192,128]{2,1,0:T(8,128)(2,1)S(1)}, u32[]{:S(2)}, u32[]{:S(2)}) collective-permute-start(bf16[3,192,128]{2,1,0:T(8,128)(2,1)S(1)} %get-tuple-element.28), channel_id=1, source_target_pairs={{0,8},{8,0},{16,24},{24,16},{1,9},{9,1},{17,25},{25,17},{2,10},{10... | collective-permute-start | bytes 442376 | tf_op jit(solution)/shard_map/ppermute | solution.py:224
where the time goes:
time: 33.5 us; the launch traced here: 33.1 us
  starting transfers between devices  14.5 us (43%)
  waiting for transfers between devices  12.5 us (37%)
  Pallas kernels  5.34 us (16%)
  between operations  0.68 us (2%)
    ppermute x10, starting transfers between devices, exchange(): return lax.ppermute(block, ('tm', 'height'), pairs)  13.9 us
    ppermute x10, waiting for transfers between devices, exchange(): return lax.ppermute(block, ('tm', 'height'), pairs)  10 us
    pallas_call x1, Pallas kernels, body(): call(functools.partial(main_kernel, tok, chips, heights, sides, scale), [...  3.17 us
    ppermute x2, waiting for transfers between devices, swap_cores(): return lax.ppermute(block, 'tm', [(t, t ^ 1) for t in range(times)])  2.5 us
    pallas_call x1, Pallas kernels, body(): call(functools.partial(pack_kernel, tok), [packed, packed], [HBM] * 6, [p...  1.12 us
    pallas_call x1, Pallas kernels, body(): call(functools.partial(final_kernel, tok), [(queries.shape, bf16)] * 3, [...  0.74 us
  transfers between devices with their start and end apart: 12, of which 5 were waited for; matrix products, arithmetic and copies ran while one was open for 0% of the time, Pallas kernels for 0%

commit v1 on v0

v1 whole, which is shorter than its diff:
```python
import functools

import jax
import jax.numpy as jnp
from jax import lax
from jax.experimental import pallas as pl
from jax.experimental.pallas import tpu as pltpu
from jax.sharding import PartitionSpec as P

VMEM = pl.BlockSpec(memory_space=pltpu.VMEM)
HBM = pl.BlockSpec(memory_space=pltpu.HBM)
LIMIT = pltpu.CompilerParams(vmem_limit_bytes=32 * 1024 * 1024)
ROWS_T = (((1,), (1,)), ((), ()))
COLS_T = (((0,), (0,)), ((), ()))


def dot(a, b, dims=(((1,), (0,)), ((), ()))):
    return lax.dot_general(a, b, dims, preferred_element_type=jnp.float32)


def place():
    t = lax.axis_index("tm")
    return t // 2, t % 2, lax.axis_index("height")


def pair(index, which):
    rising = (index % 2) == (0 if which == 0 else 1)
    return rising, jnp.where(rising, index + 1, index - 1)


def within(index, size):
    return (index >= 0) & (index < size)


def pack_kernel(tok, k_ref, v_ref, q_ref, g_ref, o_ref, mask_ref, kv_ref, rest_ref, other_ref, flags, sems):
    _, c, _ = place()
    copies = [pltpu.make_async_copy(mask_ref, flags, sems.at[10])]
    for i, ref in enumerate((k_ref, v_ref, q_ref, g_ref, o_ref)):
        own = kv_ref.at[i] if i < 2 else rest_ref.at[pl.ds((i - 2) * tok, tok), :]
        copies.append(pltpu.make_async_copy(ref.at[0, 0, c, 0], own, sems.at[2 * i + 1]))
        copies.append(
            pltpu.make_async_copy(ref.at[0, 0, 1 - c, 0], other_ref.at[pl.ds(i * tok, tok), :], sems.at[2 * i])
        )
    for copy in copies:
        copy.start()
    copies[0].wait()
    row = lax.broadcasted_iota(jnp.int32, (16, rest_ref.shape[1]), 0)
    spread = jnp.zeros(row.shape, jnp.float32)
    for i in range(9):
        on = (flags[0, 0, 0, 9 * (i // 3) + 3 * (i % 3) + 1] != 0).astype(jnp.float32)
        spread = jnp.where(row == i, on, spread)
    rest_ref[pl.ds(3 * tok, 16), :] = spread.astype(jnp.bfloat16)
    other_ref[pl.ds(5 * tok, 16), :] = spread.astype(jnp.bfloat16)
    for copy in copies[1:]:
        copy.wait()


def line_kernel(tok, kv_ref, par_ref, par_kv_ref, *border_refs):
    y, c, _ = place()
    for i in range(2):
        block = par_ref[pl.ds(i * tok, tok), :]
        par_kv_ref[i] = block
        for which, ref in enumerate(border_refs):
            rising, _ = pair(y, which)
            ref[i] = jnp.where((c == 1) == rising, kv_ref[i], block)


def main_kernel(tok, chips, heights, sides, scale, *refs):
    rest_ref, par_ref = refs[:2]
    slots = 2 + sides
    sources, refs = refs[2 : 2 + 3 * slots][::-1], refs[2 + 3 * slots :]
    count = 3 * (1 + sides)
    results, (dq_ref, qs, gs, s_ref) = refs[:count], refs[count:]
    y, c, z = place()
    two = 2 * tok
    width = rest_ref.shape[1]
    f32, bf16 = jnp.float32, jnp.bfloat16
    first = c == 0

    def both(part):
        return jnp.concatenate(
            [rest_ref[pl.ds(part * tok, tok), :], par_ref[pl.ds((part + 2) * tok, tok), :]], axis=0
        )

    qs[...], gs[...] = both(0), both(1)
    product = both(1).astype(f32) * both(2).astype(f32)
    delta = jnp.sum(product.T, axis=0, keepdims=True)

    lane = lax.broadcasted_iota(jnp.int32, (1, width), 1)
    own_flags = rest_ref[pl.ds(3 * tok, 16), :].astype(f32)
    par_flags = par_ref[pl.ds(5 * tok, 16), :].astype(f32)
    none = jnp.zeros((1, width), f32)

    def bias(line, slot):
        inside = True
        if line:
            z_rising, z_at = pair(z, line - 1)
            inside = within(z_at, heights)

        def at(flags, dt):
            if line == 0:
                return flags[3 * dt + 1 : 3 * dt + 2] if dt != 1 else none + 1.0
            return jnp.where(z_rising, flags[3 * dt + 2 : 3 * dt + 3], flags[3 * dt : 3 * dt + 1])

        if slot == 0:
            own, par = at(own_flags, 1), jnp.where(first, at(par_flags, 0), at(par_flags, 2))
        elif slot == 1:
            own, par = jnp.where(first, at(own_flags, 2), at(own_flags, 0)), at(par_flags, 1)
        else:
            rising, y_at = pair(y, slot - 2)
            inside = within(y_at, chips) & inside
            near = first != rising
            own = jnp.where(near, jnp.where(rising, at(own_flags, 2), at(own_flags, 0)), none)
            par = jnp.where(near, none, jnp.where(rising, at(par_flags, 2), at(par_flags, 0)))
        row = jnp.concatenate([jnp.where(lane + start < tok, own, par) for start in range(0, two, width)], axis=1)
        return jnp.where(inside, (row - 1.0) * 1e30, -1e30)

    blocks = [(line, slot, pl.ds((line * slots + slot) * tok, tok)) for line in range(3) for slot in range(slots)]
    top = jnp.full((8, two), -1e30, f32)
    for line, slot, kept in blocks:
        scores = dot(sources[line * slots + slot][0], qs[...], ROWS_T) * scale + bias(line, slot)
        s_ref[kept, :] = scores
        top = jnp.maximum(top, jnp.max(scores.reshape(tok // 8, 8, two), axis=0))
    top = jnp.max(top, axis=0, keepdims=True)
    total = jnp.zeros((8, two), f32)
    for _, _, kept in blocks:
        weights = jnp.exp(s_ref[kept, :] - top)
        s_ref[kept, :] = weights
        total = total + jnp.sum(weights.reshape(tok // 8, 8, two), axis=0)
    share = 1.0 / jnp.sum(total, axis=0, keepdims=True)

    dq = jnp.zeros((two, width), f32)
    for line, slot, kept in blocks:
        source = sources[line * slots + slot]
        probs = s_ref[kept, :] * share
        grads = dot(source[1], gs[...], ROWS_T)
        low = (probs * (grads - delta) * scale).astype(bf16)
        result = results[line * (1 + sides) + max(slot - 1, 0)]
        rows = pl.ds(tok if slot == 1 else 0, tok)
        result[0, rows, :] = dot(low, qs[...]).astype(bf16)
        result[1, rows, :] = dot(probs.astype(bf16), gs[...]).astype(bf16)
        dq = dq + dot(low, source[0], COLS_T)
    dq_ref[...] = dq.astype(bf16)


def sum_kernel(tok, chips, heights, sides, *refs):
    count = 3 * (1 + sides)
    parts, (dq_ref, mine_ref, swap_ref) = refs[:count], refs[count:]
    y, c, z = place()

    def total(i, own):
        value = jnp.zeros(mine_ref.shape[1:], jnp.float32)
        for line in range(3):
            inside = True
            if line:
                _, z_at = pair(z, line - 1)
                inside = within(z_at, heights)
            block = parts[line * (1 + sides)][i, pl.ds(0 if own else tok, tok), :].astype(jnp.float32)
            value = value + (jnp.where(inside, block, 0.0) if line else block)
            for which in range(sides):
                rising, y_at = pair(y, which)
                near = ((c == 1) == rising) if own else ((c == 0) == rising)
                halo = parts[line * (1 + sides) + 1 + which][i].astype(jnp.float32)
                value = value + jnp.where(near & within(y_at, chips) & inside, halo, 0.0)
        return value

    for i in range(2):
        mine_ref[i] = total(i, True)
        swap_ref[i] = total(i, False).astype(jnp.bfloat16)
    swap_ref[2] = dq_ref[pl.ds(tok, tok), :]


def final_kernel(tok, mine_ref, swap_ref, dq_ref, gq_ref, gk_ref, gv_ref):
    _, c, _ = place()
    gq_ref[0, 0, c, 0] = dq_ref[pl.ds(0, tok), :]
    gq_ref[0, 0, 1 - c, 0] = swap_ref[2]
    for i, ref in enumerate((gk_ref, gv_ref)):
        ref[0, 0, c, 0] = mine_ref[i].astype(jnp.bfloat16)
        ref[0, 0, 1 - c, 0] = swap_ref[i]


def body(queries, keys, values, grad_out, attn_out, window_mask):
    tok, width = queries.shape[-2:]
    scale = width ** -0.5
    times, heights = lax.axis_size("tm"), lax.axis_size("height")
    chips = times // 2
    sides = 1 if chips == 2 else 2
    bf16, f32 = jnp.bfloat16, jnp.float32

    def call(kernel, shapes, specs, scratch=()):
        return pl.pallas_call(
            kernel,
            out_shape=[jax.ShapeDtypeStruct(*shape) for shape in shapes],
            in_specs=list(specs),
            out_specs=[VMEM] * len(shapes),
            scratch_shapes=list(scratch),
            compiler_params=LIMIT,
        )

    def partner(index, which, size):
        if which is None:
            return index
        at = index + 1 if index % 2 == which else index - 1
        return at if 0 <= at < size else None

    def exchange(block, y_which, z_which):
        pairs = []
        for t in range(times):
            for z in range(heights):
                y_at, z_at = partner(t // 2, y_which, chips), partner(z, z_which, heights)
                at = t * heights + z
                alone = y_at is None or z_at is None
                pairs.append((at, (t ^ 1) * heights + z if alone else (2 * y_at + t % 2) * heights + z_at))
        return lax.ppermute(block, ("tm", "height"), pairs)

    def swap_cores(block):
        return lax.ppermute(block, "tm", [(t, t ^ 1) for t in range(times)])

    line_shape, tile_shape = ((2, 2 * tok, width), bf16), ((2, tok, width), bf16)
    arguments = (keys, values, queries, grad_out, attn_out, window_mask)
    kv, rest, other = call(
        functools.partial(pack_kernel, tok),
        [tile_shape, ((3 * tok + 16, width), bf16), ((5 * tok + 16, width), bf16)],
        [HBM] * 6,
        [pltpu.SMEM(window_mask.shape, jnp.int32), pltpu.SemaphoreType.DMA((11,))],
    )(*(pltpu.with_memory_space_constraint(x, pltpu.HBM) for x in arguments))
    found = {(0, 0): kv}
    for j in (1, 2):
        found[j, 0] = exchange(kv, None, j - 1)
    par = swap_cores(other)
    par_kv, *borders = call(
        functools.partial(line_kernel, tok), [tile_shape] * (1 + sides), [VMEM] * 2
    )(kv, par)
    found[0, 1] = par_kv
    for j in (1, 2):
        found[j, 1] = exchange(par_kv, None, j - 1)
    for j in (2, 1, 0):
        for which in range(sides):
            found[j, 2 + which] = exchange(borders[which], which, None if j == 0 else j - 1)
    order = [(j, k) for j in range(3) for k in range(2 + sides)]
    back_order = [(j, k) for j in range(3) for k in range(1 + sides)]
    *columns, dq = call(
        functools.partial(main_kernel, tok, chips, heights, sides, scale),
        [line_shape if k == 0 else tile_shape for _, k in back_order] + [((2 * tok, width), bf16)],
        [VMEM] * (2 + len(order)),
        [
            pltpu.VMEM((2 * tok, width), bf16),
            pltpu.VMEM((2 * tok, width), bf16),
            pltpu.VMEM((3 * (2 + sides) * tok, 2 * tok), f32),
        ],
    )(rest, par, *(found[at] for at in order[::-1]))
    back = []
    for (j, k), column in zip(back_order, columns):
        y_which, z_which = None if k == 0 else k - 1, None if j == 0 else j - 1
        back.append(column if j == k == 0 else exchange(column, y_which, z_which))
    mine, leaving = call(
        functools.partial(sum_kernel, tok, chips, heights, sides),
        [((2, tok, width), f32), ((3, tok, width), bf16)],
        [VMEM] * (len(back) + 1),
    )(*back, dq)
    return call(
        functools.partial(final_kernel, tok),
        [(queries.shape, bf16)] * 3,
        [VMEM] * 3,
    )(mine, swap_cores(leaving), dq)


def solution(mesh):
    placed = P("tm", "height", "dp", None, None, None)
    return jax.shard_map(
        body,
        mesh=mesh,
        in_specs=(placed,) * 5 + (P("tm", "height", None, None),),
        out_specs=(placed,) * 3,
        check_vma=False,
    )
```

time: 33.5 us -> 30.9 us (0.922)
  waiting for transfers between devices: 12.5 us -> 8.98 us
  starting transfers between devices: 14.5 us -> 15.5 us
    ppermute x10 -> x12, waiting for transfers between devices: 10 us -> 7.62 us  [exchange(): return lax.ppermute(block, ('tm', 'height'), pairs)]
    ppermute x2, waiting for transfers between devices: 2.5 us -> 1.36 us  [swap_cores(): return lax.ppermute(block, 'tm', [(t, t ^ 1) for t in range(times)])]
    ppermute x10 -> x12, starting transfers between devices: 13.9 us -> 14.9 us  [exchange(): return lax.ppermute(block, ('tm', 'height'), pairs)]
  transfers between devices with their start and end apart: 12 -> 14, of which waited for: 5 -> 5; matrix products, arithmetic and copies ran while one was open for 0% -> 0% of each run, Pallas kernels for 0% -> 0%
where the time goes in v1:
time: 30.9 us; the launch traced here: 30.5 us
  starting transfers between devices  15.5 us (50%)
  waiting for transfers between devices  8.98 us (29%)
  Pallas kernels  5.33 us (17%)
  between operations  0.68 us (2%)
    ppermute x12, starting transfers between devices, exchange(): return lax.ppermute(block, ('tm', 'height'), pairs)  14.9 us
    ppermute x12, waiting for transfers between devices, exchange(): return lax.ppermute(block, ('tm', 'height'), pairs)  7.62 us
    pallas_call x1, Pallas kernels, body(): call(functools.partial(main_kernel, tok, chips, heights, sides, scale), [...  3.17 us
    ppermute x2, waiting for transfers between devices, swap_cores(): return lax.ppermute(block, 'tm', [(t, t ^ 1) for t in range(times)])  1.36 us
    pallas_call x1, Pallas kernels, body(): call(functools.partial(pack_kernel, tok), [tile_shape, ((3 * tok + 16, wi...  1.12 us
    pallas_call x1, Pallas kernels, body(): call(functools.partial(final_kernel, tok), [(queries.shape, bf16)] * 3, [...  0.74 us
  transfers between devices with their start and end apart: 14, of which 5 were waited for; matrix products, arithmetic and copies ran while one was open for 0% of the time, Pallas kernels for 0%

profile of v1, /device:TPU:0, one launch (start us, length us, event | category | flops | bytes accessed | tf_op | source)
XLA Modules:
  0.0 30.5 jit_solution(15665920035440997033)
XLA Ops:
  0.6 1.1 %shard_map.85 = (bf16[2,192,128]{2,1,0:T(8,128)(2,1)S(1)}, bf16[592,128]{1,0:T(8,128)(2,1)S(1)}, bf16[976,128]{1,0:T(8,128)(2,1)S(1)}) custom-call(bf16[1,1,2,1,192,128]{5,4,3,2,1,0:T(8,128)(2,1)} %k_ref.1, bf16[1,1,2,1,192,128]{5,4,3,2,1,0:T(8,128)(2,1)} %v_ref.1, bf16[1,1,2,1,192,128]{5,4,3,2,1,0:T(8,128)(2,1)} %q_ref.1, ...), custom_call_target="tpu_custom_call" | custom-call | tf_op jit(solution)/shard_map/pallas_call | solution.py:221
  1.8 0.5 %collective-permute-start = (bf16[976,128]{1,0:T(8,128)(2,1)S(1)}, bf16[976,128]{1,0:T(8,128)(2,1)S(1)}, u32[]{:S(2)}, u32[]{:S(2)}) collective-permute-start(bf16[976,128]{1,0:T(8,128)(2,1)S(1)} %get-tuple-element.18), channel_id=1, source_target_pairs={{0,8},{8,0},{16,24},{24,16},{1,9},{9,1},{17,25},{25,17},{2,10},{10... | collective-permute-start | bytes 749576 | tf_op jit(solution)/shard_map/ppermute | solution.py:217
  2.3 2.6 %collective-permute-start.6 = (bf16[2,192,128]{2,1,0:T(8,128)(2,1)S(1)}, bf16[2,192,128]{2,1,0:T(8,128)(2,1)S(1)}, u32[]{:S(2)}, u32[]{:S(2)}) collective-permute-start(bf16[2,192,128]{2,1,0:T(8,128)(2,1)S(1)} %get-tuple-element.19.kv_ref.refs_10_), channel_id=1, source_target_pairs={{0,2},{2,0},{4,6},{6,4},{8,10},{10,8},{12,14},{14,12},{16,18},{18,... | collective-permute-start | bytes 294920 | tf_op jit(solution)/shard_map/ppermute | solution.py:214
  4.9 0.2 collective-permute-start.3
  5.1 0.0 collective-permute-done.par_ref.refs_1_
  5.1 1.6 %collective-permute-start.7 = (bf16[2,192,128]{2,1,0:T(8,128)(2,1)S(1)}, bf16[2,192,128]{2,1,0:T(8,128)(2,1)S(1)}, u32[]{:S(2)}, u32[]{:S(2)}) collective-permute-start(bf16[2,192,128]{2,1,0:T(8,128)(2,1)S(1)} %get-tuple-element.20), channel_id=1, source_target_pairs={{0,16},{2,18},{4,20},{6,22},{8,24},{10,26},{12,28},{14,30},{16,0},... | collective-permute-start | bytes 294920 | tf_op jit(solution)/shard_map/ppermute | solution.py:214
  6.7 2.9 %collective-permute-start.4 = (bf16[2,192,128]{2,1,0:T(8,128)(2,1)S(1)}, bf16[2,192,128]{2,1,0:T(8,128)(2,1)S(1)}, u32[]{:S(2)}, u32[]{:S(2)}) collective-permute-start(bf16[2,192,128]{2,1,0:T(8,128)(2,1)S(1)} %get-tuple-element.20), channel_id=1, source_target_pairs={{0,18},{2,16},{4,22},{6,20},{8,26},{10,24},{12,30},{14,28},{16,2},... | collective-permute-start | bytes 294920 | tf_op jit(solution)/shard_map/ppermute | solution.py:214
  9.7 0.0 collective-permute-start.1
  9.7 0.0 collective-permute-done.6.refs_7_
  9.7 2.4 %collective-permute-start.5 = (bf16[2,192,128]{2,1,0:T(8,128)(2,1)S(1)}, bf16[2,192,128]{2,1,0:T(8,128)(2,1)S(1)}, u32[]{:S(2)}, u32[]{:S(2)}) collective-permute-start(bf16[2,192,128]{2,1,0:T(8,128)(2,1)S(1)} %get-tuple-element.21.refs_9_), channel_id=1, source_target_pairs={{0,2},{2,0},{4,6},{6,4},{8,10},{10,8},{12,14},{14,12},{16,18},{18,... | collective-permute-start | bytes 294920 | tf_op jit(solution)/shard_map/ppermute | solution.py:214
  12.1 0.0 collective-permute-done.7.refs_8_
  12.1 0.6 %collective-permute-done.4.refs_5_ = bf16[2,192,128]{2,1,0:T(8,128)(2,1)S(1)} collective-permute-done((bf16[2,192,128]{2,1,0:T(8,128)(2,1)S(1)}, bf16[2,192,128]{2,1,0:T(8,128)(2,1)S(1)}, u32[]{:S(2)}, u32[]{:S(2)}) %collective-permute-start.4) | collective-permute-done | bytes 98336 | tf_op jit(solution)/shard_map/ppermute | solution.py:214
  12.7 0.0 collective-permute-done.1.refs_2_
  12.7 2.2 %collective-permute-done.5.refs_6_ = bf16[2,192,128]{2,1,0:T(8,128)(2,1)S(1)} collective-permute-done((bf16[2,192,128]{2,1,0:T(8,128)(2,1)S(1)}, bf16[2,192,128]{2,1,0:T(8,128)(2,1)S(1)}, u32[]{:S(2)}, u32[]{:S(2)}) %collective-permute-start.5) | collective-permute-done | bytes 98336 | tf_op jit(solution)/shard_map/ppermute | solution.py:214
  14.9 3.2 %shard_map.87 = (bf16[2,384,128]{2,1,0:T(8,128)(2,1)S(1)}, bf16[2,192,128]{2,1,0:T(8,128)(2,1)S(1)}, bf16[2,384,128]{2,1,0:T(8,128)(2,1)S(1)}, bf16[2,192,128]{2...) custom-call(bf16[592,128]{1,0:T(8,128)(2,1)S(1)} %get-tuple-element., ...), custom_call_target="tpu_custom_call" | custom-call | tf_op jit(solution)/shard_map/pallas_call | solution.py:242
  18.1 2.3 %collective-permute-start.9 = (bf16[2,384,128]{2,1,0:T(8,128)(2,1)S(1)}, bf16[2,384,128]{2,1,0:T(8,128)(2,1)S(1)}, u32[]{:S(2)}, u32[]{:S(2)}) collective-permute-start(bf16[2,384,128]{2,1,0:T(8,128)(2,1)S(1)} %get-tuple-element.24), channel_id=1, source_target_pairs={{0,2},{2,0},{4,6},{6,4},{8,10},{10,8},{12,14},{14,12},{16,18},{18,... | collective-permute-start | bytes 589832 | tf_op jit(solution)/shard_map/ppermute | solution.py:214
  20.3 1.5 %collective-permute-start.8 = (bf16[2,192,128]{2,1,0:T(8,128)(2,1)S(1)}, bf16[2,192,128]{2,1,0:T(8,128)(2,1)S(1)}, u32[]{:S(2)}, u32[]{:S(2)}) collective-permute-start(bf16[2,192,128]{2,1,0:T(8,128)(2,1)S(1)} %get-tuple-element.23), channel_id=1, source_target_pairs={{0,16},{2,18},{4,20},{6,22},{8,24},{10,26},{12,28},{14,30},{16,0},... | collective-permute-start | bytes 294920 | tf_op jit(solution)/shard_map/ppermute | solution.py:214
  21.8 1.4 %collective-permute-start.10 = (bf16[2,192,128]{2,1,0:T(8,128)(2,1)S(1)}, bf16[2,192,128]{2,1,0:T(8,128)(2,1)S(1)}, u32[]{:S(2)}, u32[]{:S(2)}) collective-permute-start(bf16[2,192,128]{2,1,0:T(8,128)(2,1)S(1)} %get-tuple-element.25), channel_id=1, source_target_pairs={{0,18},{2,16},{4,22},{6,20},{8,26},{10,24},{12,30},{14,28},{16,2},... | collective-permute-start | bytes 294920 | tf_op jit(solution)/shard_map/ppermute | solution.py:214
  23.2 3.4 %collective-permute-done.8.refs_1_ = bf16[2,192,128]{2,1,0:T(8,128)(2,1)S(1)} collective-permute-done((bf16[2,192,128]{2,1,0:T(8,128)(2,1)S(1)}, bf16[2,192,128]{2,1,0:T(8,128)(2,1)S(1)}, u32[]{:S(2)}, u32[]{:S(2)}) %collective-permute-start.8) | collective-permute-done | bytes 98336 | tf_op jit(solution)/shard_map/ppermute | solution.py:214
  26.7 1.4 %collective-permute-done.10.refs_3_ = bf16[2,192,128]{2,1,0:T(8,128)(2,1)S(1)} collective-permute-done((bf16[2,192,128]{2,1,0:T(8,128)(2,1)S(1)}, bf16[2,192,128]{2,1,0:T(8,128)(2,1)S(1)}, u32[]{:S(2)}, u32[]{:S(2)}) %collective-permute-start.10) | collective-permute-done | bytes 98336 | tf_op jit(solution)/shard_map/ppermute | solution.py:214
  28.0 0.3 shard_map.88
  28.3 0.1 collective-permute-start.13
  28.4 1.4 %collective-permute-done.13.swap_ref = bf16[3,192,128]{2,1,0:T(8,128)(2,1)S(1)} collective-permute-done((bf16[3,192,128]{2,1,0:T(8,128)(2,1)S(1)}, bf16[3,192,128]{2,1,0:T(8,128)(2,1)S(1)}, u32[]{:S(2)}, u32[]{:S(2)}) %collective-permute-start.13) | collective-permute-done | bytes 147488 | tf_op jit(solution)/shard_map/ppermute | solution.py:217
  29.7 0.7 %shard_map.89 = (bf16[1,1,2,1,192,128]{5,4,3,2,1,0:T(8,128)(2,1)}, bf16[1,1,2,1,192,128]{5,4,3,2,1,0:T(8,128)(2,1)}, bf16[1,1,2,1,192,128]{5,4,3,2,1,0:T(8,128)(2,1)}) custom-call(f32[2,192,128]{2,1,0:T(8,128)S(1)} %get-tuple-element.29.mine_ref, bf16[3,192,128]{2,1,0:T(8,128)(2,1)S(1)} %collective-permute-done.13.swap_ref, ...), custom_call_target="tpu_custom_call" | custom-call | tf_op jit(solution)/shard_map/pallas_call | solution.py:261
  (9 shorter events, 0.1 us)
Async XLA Ops:
  1.8 3.3 %collective-permute-start = (bf16[976,128]{1,0:T(8,128)(2,1)S(1)}, bf16[976,128]{1,0:T(8,128)(2,1)S(1)}, u32[]{:S(2)}, u32[]{:S(2)}) collective-permute-start(bf16[976,128]{1,0:T(8,128)(2,1)S(1)} %get-tuple-element.18), channel_id=1, source_target_pairs={{0,8},{8,0},{16,24},{24,16},{1,9},{9,1},{17,25},{25,17},{2,10},{10... | collective-permute-start | bytes 749576 | tf_op jit(solution)/shard_map/ppermute | solution.py:217
  2.3 7.4 %collective-permute-start.6 = (bf16[2,192,128]{2,1,0:T(8,128)(2,1)S(1)}, bf16[2,192,128]{2,1,0:T(8,128)(2,1)S(1)}, u32[]{:S(2)}, u32[]{:S(2)}) collective-permute-start(bf16[2,192,128]{2,1,0:T(8,128)(2,1)S(1)} %get-tuple-element.19.kv_ref.refs_10_), channel_id=1, source_target_pairs={{0,2},{2,0},{4,6},{6,4},{8,10},{10,8},{12,14},{14,12},{16,18},{18,... | collective-permute-start | bytes 294920 | tf_op jit(solution)/shard_map/ppermute | solution.py:214
  4.9 7.1 %collective-permute-start.3 = (bf16[2,192,128]{2,1,0:T(8,128)(2,1)S(1)}, bf16[2,192,128]{2,1,0:T(8,128)(2,1)S(1)}, u32[]{:S(2)}, u32[]{:S(2)}) collective-permute-start(bf16[2,192,128]{2,1,0:T(8,128)(2,1)S(1)} %get-tuple-element.19.kv_ref.refs_10_), channel_id=1, source_target_pairs={{0,8},{2,4},{4,2},{6,14},{8,0},{10,12},{12,10},{14,6},{16,24},{18,... | collective-permute-start | bytes 294920 | tf_op jit(solution)/shard_map/ppermute | solution.py:214
  5.1 6.9 %collective-permute-start.7 = (bf16[2,192,128]{2,1,0:T(8,128)(2,1)S(1)}, bf16[2,192,128]{2,1,0:T(8,128)(2,1)S(1)}, u32[]{:S(2)}, u32[]{:S(2)}) collective-permute-start(bf16[2,192,128]{2,1,0:T(8,128)(2,1)S(1)} %get-tuple-element.20), channel_id=1, source_target_pairs={{0,16},{2,18},{4,20},{6,22},{8,24},{10,26},{12,28},{14,30},{16,0},... | collective-permute-start | bytes 294920 | tf_op jit(solution)/shard_map/ppermute | solution.py:214
  6.7 5.9 %collective-permute-start.4 = (bf16[2,192,128]{2,1,0:T(8,128)(2,1)S(1)}, bf16[2,192,128]{2,1,0:T(8,128)(2,1)S(1)}, u32[]{:S(2)}, u32[]{:S(2)}) collective-permute-start(bf16[2,192,128]{2,1,0:T(8,128)(2,1)S(1)} %get-tuple-element.20), channel_id=1, source_target_pairs={{0,18},{2,16},{4,22},{6,20},{8,26},{10,24},{12,30},{14,28},{16,2},... | collective-permute-start | bytes 294920 | tf_op jit(solution)/shard_map/ppermute | solution.py:214
  9.7 3.0 %collective-permute-start.1 = (bf16[2,192,128]{2,1,0:T(8,128)(2,1)S(1)}, bf16[2,192,128]{2,1,0:T(8,128)(2,1)S(1)}, u32[]{:S(2)}, u32[]{:S(2)}) collective-permute-start(bf16[2,192,128]{2,1,0:T(8,128)(2,1)S(1)} %get-tuple-element.20), channel_id=1, source_target_pairs={{0,8},{2,20},{4,18},{6,14},{8,0},{10,28},{12,26},{14,6},{16,24},{1... | collective-permute-start | bytes 294920 | tf_op jit(solution)/shard_map/ppermute | solution.py:214
  9.7 5.2 %collective-permute-start.5 = (bf16[2,192,128]{2,1,0:T(8,128)(2,1)S(1)}, bf16[2,192,128]{2,1,0:T(8,128)(2,1)S(1)}, u32[]{:S(2)}, u32[]{:S(2)}) collective-permute-start(bf16[2,192,128]{2,1,0:T(8,128)(2,1)S(1)} %get-tuple-element.21.refs_9_), channel_id=1, source_target_pairs={{0,2},{2,0},{4,6},{6,4},{8,10},{10,8},{12,14},{14,12},{16,18},{18,... | collective-permute-start | bytes 294920 | tf_op jit(solution)/shard_map/ppermute | solution.py:214
  12.1 2.8 %collective-permute-start.2 = (bf16[2,192,128]{2,1,0:T(8,128)(2,1)S(1)}, bf16[2,192,128]{2,1,0:T(8,128)(2,1)S(1)}, u32[]{:S(2)}, u32[]{:S(2)}) collective-permute-start(bf16[2,192,128]{2,1,0:T(8,128)(2,1)S(1)} %get-tuple-element.21.refs_9_), channel_id=1, source_target_pairs={{0,8},{2,4},{4,2},{6,14},{8,0},{10,12},{12,10},{14,6},{16,24},{18,... | collective-permute-start | bytes 294920 | tf_op jit(solution)/shard_map/ppermute | solution.py:214
  18.1 10.0 %collective-permute-start.9 = (bf16[2,384,128]{2,1,0:T(8,128)(2,1)S(1)}, bf16[2,384,128]{2,1,0:T(8,128)(2,1)S(1)}, u32[]{:S(2)}, u32[]{:S(2)}) collective-permute-start(bf16[2,384,128]{2,1,0:T(8,128)(2,1)S(1)} %get-tuple-element.24), channel_id=1, source_target_pairs={{0,2},{2,0},{4,6},{6,4},{8,10},{10,8},{12,14},{14,12},{16,18},{18,... | collective-permute-start | bytes 589832 | tf_op jit(solution)/shard_map/ppermute | solution.py:214
  20.3 7.7 %collective-permute-start.11 = (bf16[2,384,128]{2,1,0:T(8,128)(2,1)S(1)}, bf16[2,384,128]{2,1,0:T(8,128)(2,1)S(1)}, u32[]{:S(2)}, u32[]{:S(2)}) collective-permute-start(bf16[2,384,128]{2,1,0:T(8,128)(2,1)S(1)} %get-tuple-element.26), channel_id=1, source_target_pairs={{0,8},{2,4},{4,2},{6,14},{8,0},{10,12},{12,10},{14,6},{16,24},{18,... | collective-permute-start | bytes 589832 | tf_op jit(solution)/shard_map/ppermute | solution.py:214
  20.3 6.3 %collective-permute-start.8 = (bf16[2,192,128]{2,1,0:T(8,128)(2,1)S(1)}, bf16[2,192,128]{2,1,0:T(8,128)(2,1)S(1)}, u32[]{:S(2)}, u32[]{:S(2)}) collective-permute-start(bf16[2,192,128]{2,1,0:T(8,128)(2,1)S(1)} %get-tuple-element.23), channel_id=1, source_target_pairs={{0,16},{2,18},{4,20},{6,22},{8,24},{10,26},{12,28},{14,30},{16,0},... | collective-permute-start | bytes 294920 | tf_op jit(solution)/shard_map/ppermute | solution.py:214
  21.8 6.2 %collective-permute-start.10 = (bf16[2,192,128]{2,1,0:T(8,128)(2,1)S(1)}, bf16[2,192,128]{2,1,0:T(8,128)(2,1)S(1)}, u32[]{:S(2)}, u32[]{:S(2)}) collective-permute-start(bf16[2,192,128]{2,1,0:T(8,128)(2,1)S(1)} %get-tuple-element.25), channel_id=1, source_target_pairs={{0,18},{2,16},{4,22},{6,20},{8,26},{10,24},{12,30},{14,28},{16,2},... | collective-permute-start | bytes 294920 | tf_op jit(solution)/shard_map/ppermute | solution.py:214
  23.2 4.8 %collective-permute-start.12 = (bf16[2,192,128]{2,1,0:T(8,128)(2,1)S(1)}, bf16[2,192,128]{2,1,0:T(8,128)(2,1)S(1)}, u32[]{:S(2)}, u32[]{:S(2)}) collective-permute-start(bf16[2,192,128]{2,1,0:T(8,128)(2,1)S(1)} %get-tuple-element.27), channel_id=1, source_target_pairs={{0,8},{2,20},{4,18},{6,14},{8,0},{10,28},{12,26},{14,6},{16,24},{1... | collective-permute-start | bytes 294920 | tf_op jit(solution)/shard_map/ppermute | solution.py:214
  28.3 1.4 %collective-permute-start.13 = (bf16[3,192,128]{2,1,0:T(8,128)(2,1)S(1)}, bf16[3,192,128]{2,1,0:T(8,128)(2,1)S(1)}, u32[]{:S(2)}, u32[]{:S(2)}) collective-permute-start(bf16[3,192,128]{2,1,0:T(8,128)(2,1)S(1)} %get-tuple-element.30), channel_id=1, source_target_pairs={{0,8},{8,0},{16,24},{24,16},{1,9},{9,1},{17,25},{25,17},{2,10},{10... | collective-permute-start | bytes 442376 | tf_op jit(solution)/shard_map/ppermute | solution.py:217

commit v2 on v1

v2 whole, which is shorter than its diff:
```python
import functools

import jax
import jax.numpy as jnp
from jax import lax
from jax.experimental import pallas as pl
from jax.experimental.pallas import tpu as pltpu
from jax.sharding import PartitionSpec as P

VMEM = pl.BlockSpec(memory_space=pltpu.VMEM)
HBM = pl.BlockSpec(memory_space=pltpu.HBM)
LIMIT = pltpu.CompilerParams(vmem_limit_bytes=32 * 1024 * 1024)
ROWS_T = (((1,), (1,)), ((), ()))
COLS_T = (((0,), (0,)), ((), ()))


def dot(a, b, dims=(((1,), (0,)), ((), ()))):
    return lax.dot_general(a, b, dims, preferred_element_type=jnp.float32)


def place():
    t = lax.axis_index("tm")
    return t // 2, t % 2, lax.axis_index("height")


def pair(index, which):
    rising = (index % 2) == (0 if which == 0 else 1)
    return rising, jnp.where(rising, index + 1, index - 1)


def within(index, size):
    return (index >= 0) & (index < size)


def pack_kernel(tok, k_ref, v_ref, q_ref, g_ref, o_ref, mask_ref, kv_ref, rest_ref, other_ref, flags, sems):
    _, c, _ = place()
    copies = [pltpu.make_async_copy(mask_ref, flags, sems.at[10])]
    for i, ref in enumerate((k_ref, v_ref, q_ref, g_ref, o_ref)):
        own = kv_ref.at[i] if i < 2 else rest_ref.at[pl.ds((i - 2) * tok, tok), :]
        copies.append(pltpu.make_async_copy(ref.at[0, 0, c, 0], own, sems.at[2 * i + 1]))
        copies.append(
            pltpu.make_async_copy(ref.at[0, 0, 1 - c, 0], other_ref.at[pl.ds(i * tok, tok), :], sems.at[2 * i])
        )
    for copy in copies:
        copy.start()
    copies[0].wait()
    row = lax.broadcasted_iota(jnp.int32, (16, rest_ref.shape[1]), 0)
    spread = jnp.zeros(row.shape, jnp.float32)
    for i in range(9):
        on = (flags[0, 0, 0, 9 * (i // 3) + 3 * (i % 3) + 1] != 0).astype(jnp.float32)
        spread = jnp.where(row == i, on, spread)
    rest_ref[pl.ds(3 * tok, 16), :] = spread.astype(jnp.bfloat16)
    other_ref[pl.ds(5 * tok, 16), :] = spread.astype(jnp.bfloat16)
    for copy in copies[1:]:
        copy.wait()


def rows_at(index, tok):
    return pl.ds(index * tok, tok)


def border_is_own(y, c):
    rising, _ = pair(y, 0)
    return (c == 1) == rising


def pick(near, which, own, par):
    return jnp.where(near, own, par) if which == 0 else jnp.where(near, par, own)


def line_kernel(tok, rest_ref, par_ref, par_kv_ref, *border_refs):
    y, c, _ = place()
    near = border_is_own(y, c)
    for i in range(2):
        par_kv_ref[i] = par_ref[rows_at(i, tok), :]
    for which, ref in enumerate(border_refs):
        for part in range(2):
            rows = rows_at(part, tok)
            ref[rows, :] = pick(near, which, rest_ref[rows, :], par_ref[rows_at(part + 2, tok), :])
        ref[pl.ds(2 * tok, 16), :] = pick(
            near, which, rest_ref[pl.ds(3 * tok, 16), :], par_ref[pl.ds(5 * tok, 16), :]
        )


def line_place(z, line, heights):
    if line == 0:
        return True, lambda flags, dt: flags[3 * dt + 1 : 3 * dt + 2]
    rising, at = pair(z, line - 1)
    return within(at, heights), lambda flags, dt: jnp.where(
        rising, flags[3 * dt + 2 : 3 * dt + 3], flags[3 * dt : 3 * dt + 1]
    )


def lanes_of(tok, border, other):
    width = border.shape[1]
    lane = lax.broadcasted_iota(jnp.int32, (1, width), 1)
    return jnp.concatenate(
        [jnp.where(lane + start < tok, border, other) for start in range(0, 2 * tok, width)], axis=1
    )


def first_kernel(tok, heights, scale, kv_ref, par_kv_ref, rest_ref, par_ref, qg, table, s_ref, d_ref):
    y, c, z = place()
    two = 2 * tok
    f32 = jnp.float32
    first, near = c == 0, border_is_own(y, c)
    out = []
    for part in range(3):
        own, par = rest_ref[rows_at(part, tok), :], par_ref[rows_at(part + 2, tok), :]
        tiles = [pick(near, which, own, par) for which in range(2)]
        if part == 2:
            out = jnp.concatenate(tiles, axis=0)
        else:
            for which in range(2):
                qg[part, rows_at(which, tok), :] = tiles[which]
    delta = jnp.sum((qg[1].astype(f32) * out.astype(f32)).T, axis=0, keepdims=True)

    own_flags = rest_ref[pl.ds(3 * tok, 16), :].astype(f32)
    par_flags = par_ref[pl.ds(5 * tok, 16), :].astype(f32)
    lines = []
    for line in range(3):
        inside, at = line_place(z, line, heights)
        centre = jnp.ones_like(own_flags[0:1]) if line == 0 else None
        for slot in range(2):
            if slot == 0:
                own, par = at(own_flags, 1), jnp.where(first, at(par_flags, 0), at(par_flags, 2))
            else:
                own, par = jnp.where(first, at(own_flags, 2), at(own_flags, 0)), at(par_flags, 1)
            if line == 0:
                own, par = (centre, par) if slot == 0 else (own, centre)
            row = lanes_of(tok, pick(near, 0, own, par), pick(near, 1, own, par))
            lines.append(jnp.where(inside, (row - 1.0) * 1e30, -1e30))
    table[...] = jnp.concatenate(lines + [delta, jnp.zeros((1, two), f32)], axis=0)
    for i, source in enumerate((kv_ref, par_kv_ref)):
        rows = rows_at(i, tok)
        s_ref[rows, :] = dot(source[0], qg[0], ROWS_T) * scale + table[i : i + 1, :]
        d_ref[rows, :] = dot(source[1], qg[1], ROWS_T) - table[6:7, :]


def early_kernel(tok, scale, qg, table, one_ref, two_ref, s_ref, d_ref):
    for i, source in enumerate((one_ref, two_ref)):
        rows = rows_at(i, tok)
        s_ref[rows, :] = dot(source[0], qg[0], ROWS_T) * scale + table[2 + 2 * i : 3 + 2 * i, :]
        d_ref[rows, :] = dot(source[1], qg[1], ROWS_T) - table[6:7, :]


def foreign_rows(ref, part, which, tok):
    block = ref[rows_at(part, tok), :]
    return jnp.concatenate([block, jnp.zeros_like(block)] if which == 0 else [jnp.zeros_like(block), block], axis=0)


def score_kernel(tok, chips, heights, sides, scale, qg, table, s_own, s_early, *refs):
    keys, foreign, refs = refs[:6], refs[6 : 6 + sides], refs[6 + sides :]
    s_late, s_far, *notes = refs
    y, c, z = place()
    near = border_is_own(y, c)
    two = 2 * tok
    f32 = jnp.float32
    eighths = (tok // 8, 8, two)

    def summed(blocks):
        top = jnp.full((8, two), -1e30, f32)
        for ref, i in blocks:
            top = jnp.maximum(top, jnp.max(ref[rows_at(i, tok), :].reshape(eighths), axis=0))
        top = jnp.max(top, axis=0, keepdims=True)
        total = jnp.zeros((8, two), f32)
        for ref, i in blocks:
            total = total + jnp.sum(jnp.exp(ref[rows_at(i, tok), :] - top).reshape(eighths), axis=0)
        return [top, jnp.sum(total, axis=0, keepdims=True)]

    far = []
    for which in range(sides):
        rising, y_at = pair(y, which)
        flags = foreign[which][pl.ds(2 * tok, 16), :].astype(f32)
        queries = foreign_rows(foreign[which], 0, which, tok)
        for line in range(3):
            inside, at = line_place(z, line, heights)
            row = jnp.where(rising, at(flags, 0), at(flags, 2))
            none = jnp.zeros_like(row)
            row = lanes_of(tok, *((row, none) if which == 0 else (none, row)))
            bias = jnp.where(inside & within(y_at, chips), (row - 1.0) * 1e30, -1e30)
            border = pick(near, which, keys[2 * line][0], keys[2 * line + 1][0])
            s_far[rows_at(3 * which + line, tok), :] = dot(border, queries, ROWS_T) * scale + bias
        far.append(summed([(s_far, 3 * which + line) for line in range(3)]))
    for i in range(2):
        s_late[rows_at(i, tok), :] = dot(keys[3 + 2 * i][0], qg[0], ROWS_T) * scale + table[3 + 2 * i : 4 + 2 * i, :]
    mine = summed([(ref, i) for ref in (s_own, s_early, s_late) for i in range(2)])
    for which in range(sides):
        notes[which][...] = jnp.concatenate(mine + far[which] + [table[6:7, :], jnp.zeros((3, two), f32)], axis=0)


def late_kernel(tok, sides, qg, table, *refs):
    values, foreign, (d_late, d_far) = refs[:6], refs[6 : 6 + sides], refs[6 + sides :]
    y, c, _ = place()
    near = border_is_own(y, c)
    for i in range(2):
        d_late[rows_at(i, tok), :] = dot(values[3 + 2 * i][1], qg[1], ROWS_T) - table[6:7, :]
    for which in range(sides):
        grads = foreign_rows(foreign[which], 1, which, tok)
        for line in range(3):
            border = pick(near, which, values[2 * line][1], values[2 * line + 1][1])
            d_far[rows_at(3 * which + line, tok), :] = dot(border, grads, ROWS_T)


def column_sums(low, probs, qg, far):
    sums = [dot(low, qg[0]), dot(probs, qg[1])]
    for (far_low, far_probs, queries, grads), mine in far:
        sums[0] = sums[0] + jnp.where(mine, dot(far_low, queries), 0.0)
        sums[1] = sums[1] + jnp.where(mine, dot(far_probs, grads), 0.0)
    return sums


def leave_kernel(tok, chips, sides, scale, qg, s_early, d_early, s_late, d_late, s_far, d_far, *refs):
    sent, came, foreign = (refs[i * sides : (i + 1) * sides] for i in range(3))
    one_ref, two_ref, low_ref, low_far, lse_ref = refs[3 * sides :]
    y, c, _ = place()
    near = border_is_own(y, c)
    f32, bf16 = jnp.float32, jnp.bfloat16

    def joined(top, total, other_top, other_total):
        both = jnp.maximum(top, other_top)
        return both, total * jnp.exp(top - both) + other_total * jnp.exp(other_top - both)

    top, total = sent[0][0:1, :], sent[0][1:2, :]
    table = []
    for which in range(sides):
        _, y_at = pair(y, which)
        inside = within(y_at, chips)
        note = came[which]
        top, total = joined(
            top, total, jnp.where(inside, note[2:3, :], -1e30), jnp.where(inside, note[3:4, :], 0.0)
        )
        far_top, far_total = joined(note[0:1, :], note[1:2, :], sent[which][2:3, :], sent[which][3:4, :])
        table += [jnp.where(inside, far_top + jnp.log(far_total), 0.0), jnp.where(inside, note[4:5, :], 0.0)]
    lines = [top + jnp.log(total)] + table
    lse_ref[...] = jnp.concatenate(lines + [jnp.zeros((8 - len(lines), 2 * tok), f32)], axis=0)

    queries = [foreign_rows(ref, 0, which, tok) for which, ref in enumerate(foreign)]
    grads = [foreign_rows(ref, 1, which, tok) for which, ref in enumerate(foreign)]
    for line, result in ((1, one_ref), (2, two_ref)):
        far = []
        for which in range(sides):
            rows = rows_at(3 * which + line, tok)
            probs = jnp.exp(s_far[rows, :] - lse_ref[1 + 2 * which : 2 + 2 * which, :])
            low = (probs * (d_far[rows, :] - lse_ref[2 + 2 * which : 3 + 2 * which, :]) * scale).astype(bf16)
            low_far[rows_at(2 * which + line - 1, tok), :] = low
            far.append((low, probs.astype(bf16), queries[which], grads[which]))
        for slot, (s_ref, d_ref) in enumerate(((s_early, d_early), (s_late, d_late))):
            rows = rows_at(line - 1, tok)
            probs = jnp.exp(s_ref[rows, :] - lse_ref[0:1, :])
            low = (probs * d_ref[rows, :] * scale).astype(bf16)
            low_ref[rows_at(2 * (line - 1) + slot, tok), :] = low
            owns = [(far[which], near == ((slot == 0) == (which == 0))) for which in range(sides)]
            sums = column_sums(low, probs.astype(bf16), qg, owns)
            for i in range(2):
                result[i, rows_at(slot, tok), :] = sums[i].astype(bf16)


def stay_kernel(tok, sides, scale, qg, s_own, d_own, s_far, d_far, low_ref, low_far, lse_ref, *refs):
    keys, foreign, (own_ref, dq_ref, *back_refs) = refs[:6], refs[6 : 6 + sides], refs[6 + sides :]
    y, c, _ = place()
    near = border_is_own(y, c)
    bf16 = jnp.bfloat16
    far = []
    for which in range(sides):
        rows = rows_at(3 * which, tok)
        probs = jnp.exp(s_far[rows, :] - lse_ref[1 + 2 * which : 2 + 2 * which, :])
        low = (probs * (d_far[rows, :] - lse_ref[2 + 2 * which : 3 + 2 * which, :]) * scale).astype(bf16)
        parts = [foreign_rows(foreign[which], part, which, tok) for part in range(2)]
        far.append((low, probs.astype(bf16), *parts))
        dq = dot(pick(near, which, keys[0][0], keys[1][0]), low, COLS_T)
        for line in (1, 2):
            border = pick(near, which, keys[2 * line][0], keys[2 * line + 1][0])
            dq = dq + dot(border, low_far[rows_at(2 * which + line - 1, tok), :], COLS_T)
        back_refs[which][...] = dq.T[which * tok : (which + 1) * tok].astype(bf16)
    dq = jnp.zeros(dq_ref.shape[::-1], jnp.float32)
    for slot in range(2):
        rows = rows_at(slot, tok)
        probs = jnp.exp(s_own[rows, :] - lse_ref[0:1, :])
        low = (probs * d_own[rows, :] * scale).astype(bf16)
        owns = [(far[which], near == ((slot == 0) == (which == 0))) for which in range(sides)]
        sums = column_sums(low, probs.astype(bf16), qg, owns)
        for i in range(2):
            own_ref[i, rows, :] = sums[i].astype(bf16)
        dq = dq + dot(keys[slot][0], low, COLS_T)
    for i in range(4):
        dq = dq + dot(keys[2 + i][0], low_ref[rows_at(i, tok), :], COLS_T)
    dq_ref[...] = dq.T


def sum_kernel(tok, chips, heights, sides, own_ref, one_ref, two_ref, dq_ref, *refs):
    backs, (mine_ref, mine_q_ref, swap_ref) = refs[:sides], refs[sides:]
    y, c, z = place()
    near = border_is_own(y, c)
    f32, bf16 = jnp.float32, jnp.bfloat16
    for i in range(2):
        for slot in range(2):
            rows = rows_at(slot, tok)
            value = own_ref[i, rows, :].astype(f32)
            for line, ref in ((1, one_ref), (2, two_ref)):
                inside, _ = line_place(z, line, heights)
                value = value + jnp.where(inside, ref[i, rows, :].astype(f32), 0.0)
            if slot == 0:
                mine_ref[i] = value.astype(bf16)
            else:
                swap_ref[i] = value.astype(bf16)
    tiles = []
    for tile in range(2):
        value = dq_ref[rows_at(tile, tok), :]
        if tile < sides:
            _, y_at = pair(y, tile)
            value = value + jnp.where(within(y_at, chips), backs[tile][...].astype(f32), 0.0)
        tiles.append(value.astype(bf16))
    mine_q_ref[...] = jnp.where(near, tiles[0], tiles[1])
    swap_ref[2] = jnp.where(near, tiles[1], tiles[0])


def final_kernel(mine_ref, swap_ref, mine_q_ref, gq_ref, gk_ref, gv_ref):
    _, c, _ = place()
    gq_ref[0, 0, c, 0] = mine_q_ref[...]
    gq_ref[0, 0, 1 - c, 0] = swap_ref[2]
    for i, ref in enumerate((gk_ref, gv_ref)):
        ref[0, 0, c, 0] = mine_ref[i]
        ref[0, 0, 1 - c, 0] = swap_ref[i]


def body(queries, keys, values, grad_out, attn_out, window_mask):
    tok, width = queries.shape[-2:]
    scale = width ** -0.5
    times, heights = lax.axis_size("tm"), lax.axis_size("height")
    chips = times // 2
    sides = 1 if chips == 2 else 2
    bf16, f32 = jnp.bfloat16, jnp.float32

    def call(kernel, shapes, specs, scratch=()):
        return pl.pallas_call(
            kernel,
            out_shape=[jax.ShapeDtypeStruct(*shape) for shape in shapes],
            in_specs=list(specs),
            out_specs=[VMEM] * len(shapes),
            scratch_shapes=list(scratch),
            compiler_params=LIMIT,
        )

    def partner(index, which, size):
        if which is None:
            return index
        at = index + 1 if index % 2 == which else index - 1
        return at if 0 <= at < size else None

    def exchange(block, y_which, z_which):
        pairs = []
        for t in range(times):
            for z in range(heights):
                y_at, z_at = partner(t // 2, y_which, chips), partner(z, z_which, heights)
                at = t * heights + z
                alone = y_at is None or z_at is None
                pairs.append((at, (t ^ 1) * heights + z if alone else (2 * y_at + t % 2) * heights + z_at))
        return lax.ppermute(block, ("tm", "height"), pairs)

    def swap_cores(block):
        return lax.ppermute(block, "tm", [(t, t ^ 1) for t in range(times)])

    line_shape, tile_shape = ((2, 2 * tok, width), bf16), ((2, tok, width), bf16)
    arguments = (keys, values, queries, grad_out, attn_out, window_mask)
    kv, rest, other = call(
        functools.partial(pack_kernel, tok),
        [tile_shape, ((3 * tok + 16, width), bf16), ((5 * tok + 16, width), bf16)],
        [HBM] * 6,
        [pltpu.SMEM(window_mask.shape, jnp.int32), pltpu.SemaphoreType.DMA((11,))],
    )(*(pltpu.with_memory_space_constraint(x, pltpu.HBM) for x in arguments))
    early = [exchange(kv, None, which) for which in range(2)]
    par = swap_cores(other)
    border_shape, two = ((2 * tok + 16, width), bf16), 2 * tok
    par_kv, *borders = call(
        functools.partial(line_kernel, tok), [tile_shape] + [border_shape] * sides, [VMEM] * 2
    )(rest, par)
    foreign = [exchange(borders[which], which, None) for which in range(sides)]
    late = [exchange(par_kv, None, which) for which in range(2)]
    tiles = (kv, par_kv, early[0], late[0], early[1], late[1])

    def square(count, kind=f32):
        return ((count * tok, two), kind)

    qg, table, s_own, d_own = call(
        functools.partial(first_kernel, tok, heights, scale),
        [((2, two, width), bf16), ((8, two), f32), square(2), square(2)],
        [VMEM] * 4,
    )(kv, par_kv, rest, par)
    s_early, d_early = call(
        functools.partial(early_kernel, tok, scale), [square(2), square(2)], [VMEM] * 4
    )(qg, table, *early)
    s_late, s_far, *sent = call(
        functools.partial(score_kernel, tok, chips, heights, sides, scale),
        [square(2), square(3 * sides)] + [((8, two), f32)] * sides,
        [VMEM] * (10 + sides),
    )(qg, table, s_own, s_early, *tiles, *foreign)
    came = [exchange(sent[which], which, None) for which in range(sides)]
    d_late, d_far = call(
        functools.partial(late_kernel, tok, sides), [square(2), square(3 * sides)], [VMEM] * (8 + sides)
    )(qg, table, *tiles, *foreign)
    one, other_one, low, low_far, lse = call(
        functools.partial(leave_kernel, tok, chips, sides, scale),
        [line_shape, line_shape, square(4, bf16), square(2 * sides, bf16), ((8, two), f32)],
        [VMEM] * (7 + 3 * sides),
    )(qg, s_early, d_early, s_late, d_late, s_far, d_far, *sent, *came, *foreign)
    back = [exchange(block, None, which) for which, block in enumerate((one, other_one))]
    own, dq, *shares = call(
        functools.partial(stay_kernel, tok, sides, scale),
        [line_shape, ((two, width), f32)] + [((tok, width), bf16)] * sides,
        [VMEM] * (14 + sides),
    )(qg, s_own, d_own, s_far, d_far, low, low_far, lse, *tiles, *foreign)
    shares = [exchange(share, which, None) for which, share in enumerate(shares)]
    mine, mine_q, leaving = call(
        functools.partial(sum_kernel, tok, chips, heights, sides),
        [tile_shape, ((tok, width), bf16), ((3, tok, width), bf16)],
        [VMEM] * (4 + sides),
    )(own, *back, dq, *shares)
    return call(final_kernel, [(queries.shape, bf16)] * 3, [VMEM] * 3)(mine, swap_cores(leaving), mine_q)


def solution(mesh):
    placed = P("tm", "height", "dp", None, None, None)
    return jax.shard_map(
        body,
        mesh=mesh,
        in_specs=(placed,) * 5 + (P("tm", "height", None, None),),
        out_specs=(placed,) * 3,
        check_vma=False,
    )
```

time: 30.9 us -> 29.4 us (0.951)
  starting transfers between devices: 15.5 us -> 11 us
  waiting for transfers between devices: 8.98 us -> 11.9 us
  Pallas kernels: 5.33 us -> 5.65 us
    ppermute x12 -> x9, starting transfers between devices: 14.9 us -> 10.4 us  [exchange(): return lax.ppermute(block, ('tm', 'height'), pairs)]
    ppermute x12 -> x9, waiting for transfers between devices: 7.62 us -> 9.38 us  [exchange(): return lax.ppermute(block, ('tm', 'height'), pairs)]
    ppermute x2, waiting for transfers between devices: 1.36 us -> 2.5 us  [swap_cores(): return lax.ppermute(block, 'tm', [(t, t ^ 1) for t in range(times)])]
    pallas_call x4 -> x9, Pallas kernels: 4.21 us -> 4.53 us  [the longest x1 0.86 us: body(): call(functools.partial(stay_kernel, tok, sides, scale), [line_shape, ((tw...]
  transfers between devices with their start and end apart: 14 -> 11, of which waited for: 5 -> 6; matrix products, arithmetic and copies ran while one was open for 0% -> 0% of each run, Pallas kernels for 0% -> 7%
where the time goes in v2:
time: 29.4 us; the launch traced here: 29.2 us
  waiting for transfers between devices  11.9 us (40%)
  starting transfers between devices  11 us (37%)
  Pallas kernels  5.65 us (19%)
  between operations  0.72 us (2%)
    ppermute x9, starting transfers between devices, exchange(): return lax.ppermute(block, ('tm', 'height'), pairs)  10.4 us
    ppermute x9, waiting for transfers between devices, exchange(): return lax.ppermute(block, ('tm', 'height'), pairs)  9.38 us
    ppermute x2, waiting for transfers between devices, swap_cores(): return lax.ppermute(block, 'tm', [(t, t ^ 1) for t in range(times)])  2.5 us
    pallas_call x1, Pallas kernels, body(): call(functools.partial(pack_kernel, tok), [tile_shape, ((3 * tok + 16, wi...  1.12 us
    pallas_call x1, Pallas kernels, body(): call(functools.partial(stay_kernel, tok, sides, scale), [line_shape, ((tw...  0.86 us
    pallas_call x1, Pallas kernels, body(): call(functools.partial(leave_kernel, tok, chips, sides, scale), [line_sha...  0.86 us
    pallas_call x1, Pallas kernels, body(): call(functools.partial(score_kernel, tok, chips, heights, sides, scale),...  0.82 us
    pallas_call x1, Pallas kernels, body(): call(final_kernel, [(queries.shape, bf16)] * 3, [VMEM] * 3)  0.74 us
  transfers between devices with their start and end apart: 11, of which 6 were waited for; matrix products, arithmetic and copies ran while one was open for 0% of the time, Pallas kernels for 7%

profile of v2, /device:TPU:0, one launch (start us, length us, event | category | flops | bytes accessed | tf_op | source)
XLA Modules:
  0.0 29.2 jit_solution(434285797015752533)
XLA Ops:
  0.6 1.1 %shard_map.85 = (bf16[2,192,128]{2,1,0:T(8,128)(2,1)S(1)}, bf16[592,128]{1,0:T(8,128)(2,1)S(1)}, bf16[976,128]{1,0:T(8,128)(2,1)S(1)}) custom-call(bf16[1,1,2,1,192,128]{5,4,3,2,1,0:T(8,128)(2,1)} %k_ref.1, bf16[1,1,2,1,192,128]{5,4,3,2,1,0:T(8,128)(2,1)} %v_ref.1, bf16[1,1,2,1,192,128]{5,4,3,2,1,0:T(8,128)(2,1)} %q_ref.1, ...), custom_call_target="tpu_custom_call" | custom-call | tf_op jit(solution)/shard_map/pallas_call | solution.py:366
  1.8 0.5 %collective-permute-start = (bf16[976,128]{1,0:T(8,128)(2,1)S(1)}, bf16[976,128]{1,0:T(8,128)(2,1)S(1)}, u32[]{:S(2)}, u32[]{:S(2)}) collective-permute-start(bf16[976,128]{1,0:T(8,128)(2,1)S(1)} %get-tuple-element.32), channel_id=1, source_target_pairs={{0,8},{8,0},{16,24},{24,16},{1,9},{9,1},{17,25},{25,17},{2,10},{10... | collective-permute-start | bytes 749576 | tf_op jit(solution)/shard_map/ppermute | solution.py:362
  2.3 1.1 %collective-permute-done.par_ref = bf16[976,128]{1,0:T(8,128)(2,1)S(1)} collective-permute-done((bf16[976,128]{1,0:T(8,128)(2,1)S(1)}, bf16[976,128]{1,0:T(8,128)(2,1)S(1)}, u32[]{:S(2)}, u32[]{:S(2)}) %collective-permute-start) | collective-permute-done | bytes 249888 | tf_op jit(solution)/shard_map/ppermute | solution.py:362
  3.5 3.0 %collective-permute-start.5 = (bf16[400,128]{1,0:T(8,128)(2,1)S(1)}, bf16[400,128]{1,0:T(8,128)(2,1)S(1)}, u32[]{:S(2)}, u32[]{:S(2)}) collective-permute-start(bf16[400,128]{1,0:T(8,128)(2,1)S(1)} %get-tuple-element.39), channel_id=1, source_target_pairs={{0,16},{2,18},{4,20},{6,22},{8,24},{10,26},{12,28},{14,30},{16,0},... | collective-permute-start | bytes 307208 | tf_op jit(solution)/shard_map/ppermute | solution.py:359
  6.4 3.1 %collective-permute-start.1 = (bf16[2,192,128]{2,1,0:T(8,128)(2,1)S(1)}, bf16[2,192,128]{2,1,0:T(8,128)(2,1)S(1)}, u32[]{:S(2)}, u32[]{:S(2)}) collective-permute-start(bf16[2,192,128]{2,1,0:T(8,128)(2,1)S(1)} %get-tuple-element.30.kv_ref.refs_0_), channel_id=1, source_target_pairs={{0,2},{2,0},{4,6},{6,4},{8,10},{10,8},{12,14},{14,12},{16,18},{18,... | collective-permute-start | bytes 294920 | tf_op jit(solution)/shard_map/ppermute | solution.py:359
  9.6 0.0 collective-permute-start.4
  9.6 1.6 %collective-permute-start.3 = (bf16[2,192,128]{2,1,0:T(8,128)(2,1)S(1)}, bf16[2,192,128]{2,1,0:T(8,128)(2,1)S(1)}, u32[]{:S(2)}, u32[]{:S(2)}) collective-permute-start(bf16[2,192,128]{2,1,0:T(8,128)(2,1)S(1)} %get-tuple-element.33.par_kv_ref.refs_1_), channel_id=1, source_target_pairs={{0,2},{2,0},{4,6},{6,4},{8,10},{10,8},{12,14},{14,12},{16,18},{18,... | collective-permute-start | bytes 294920 | tf_op jit(solution)/shard_map/ppermute | solution.py:359
  11.2 0.4 %shard_map.87 = (bf16[2,384,128]{2,1,0:T(8,128)(2,1)S(1)}, f32[8,384]{1,0:T(8,128)S(1)}, f32[384,384]{1,0:T(8,128)S(1)}, f32[384,384]{1,0:T(8,128)S(1)}) custom-call(bf16[2,192,128]{2,1,0:T(8,128)(2,1)S(1)} %get-tuple-element.30.kv_ref.refs_0_, bf16[2,192,128]{2,1,0:T(8,128)(2,1)S(1)} %get-tuple-element.33.par_kv_ref.refs_1_, ...), custom_call_target="tpu_custom_call" | custom-call | tf_op jit(solution)/shard_map/pallas_call | solution.py:385
  11.5 0.7 %collective-permute-done.1.one_ref.refs_2_ = bf16[2,192,128]{2,1,0:T(8,128)(2,1)S(1)} collective-permute-done((bf16[2,192,128]{2,1,0:T(8,128)(2,1)S(1)}, bf16[2,192,128]{2,1,0:T(8,128)(2,1)S(1)}, u32[]{:S(2)}, u32[]{:S(2)}) %collective-permute-start.1) | collective-permute-done | bytes 98336 | tf_op jit(solution)/shard_map/ppermute | solution.py:359
  12.3 0.3 %shard_map.88 = (f32[384,384]{1,0:T(8,128)S(1)}, f32[384,384]{1,0:T(8,128)S(1)}) custom-call(bf16[2,384,128]{2,1,0:T(8,128)(2,1)S(1)} %get-tuple-element.34.qg, f32[8,384]{1,0:T(8,128)S(1)} %get-tuple-element.37.table, bf16[2,192,128]{2,1,0:T(8,128)(2,1)S(1)} %collective-permute-done.1.one_ref.refs_2_, ...), custom_call_target="tpu_custom_call" | custom-call | tf_op jit(solution)/shard_map/pallas_call | solution.py:390
  12.6 2.2 %collective-permute-done.3.refs_3_ = bf16[2,192,128]{2,1,0:T(8,128)(2,1)S(1)} collective-permute-done((bf16[2,192,128]{2,1,0:T(8,128)(2,1)S(1)}, bf16[2,192,128]{2,1,0:T(8,128)(2,1)S(1)}, u32[]{:S(2)}, u32[]{:S(2)}) %collective-permute-start.3) | collective-permute-done | bytes 98336 | tf_op jit(solution)/shard_map/ppermute | solution.py:359
  14.8 0.8 %shard_map.89 = (f32[384,384]{1,0:T(8,128)S(1)}, f32[576,384]{1,0:T(8,128)S(1)}, f32[8,384]{1,0:T(8,128)S(1)}) custom-call(bf16[2,384,128]{2,1,0:T(8,128)(2,1)S(1)} %get-tuple-element.34.qg, f32[8,384]{1,0:T(8,128)S(1)} %get-tuple-element.37.table, f32[384,384]{1,0:T(8,128)S(1)} %get-tuple-element.35.s_own, f32[384,384]{1,0:T(8,128)S(1)} %get-tuple-element.38.s_early, ...), custom_call_target="tpu_custom_call" | custom-call | tf_op jit(solution)/shard_map/pallas_call | solution.py:393
  15.6 0.6 %collective-permute-start.6 = (f32[8,384]{1,0:T(8,128)S(1)}, f32[8,384]{1,0:T(8,128)S(1)}, u32[]{:S(2)}, u32[]{:S(2)}) collective-permute-start(f32[8,384]{1,0:T(8,128)S(1)} %get-tuple-element.45.refs_0_), channel_id=1, source_target_pairs={{0,16},{2,18},{4,20},{6,22},{8,24},{10,26},{12,28},{14,30},{16,0},... | collective-permute-start | bytes 36872 | tf_op jit(solution)/shard_map/ppermute | solution.py:359
  16.2 0.4 %shard_map.90 = (f32[384,384]{1,0:T(8,128)S(1)}, f32[576,384]{1,0:T(8,128)S(1)}) custom-call(bf16[2,384,128]{2,1,0:T(8,128)(2,1)S(1)} %get-tuple-element.34.qg, f32[8,384]{1,0:T(8,128)S(1)} %get-tuple-element.37.table, bf16[2,192,128]{2,1,0:T(8,128)(2,1)S(1)} %get-tuple-element.30.kv_ref.refs_0_, ...), custom_call_target="tpu_custom_call" | custom-call | tf_op jit(solution)/shard_map/pallas_call | solution.py:399
  16.6 2.8 %collective-permute-done.6.refs_1_ = f32[8,384]{1,0:T(8,128)S(1)} collective-permute-done((f32[8,384]{1,0:T(8,128)S(1)}, f32[8,384]{1,0:T(8,128)S(1)}, u32[]{:S(2)}, u32[]{:S(2)}) %collective-permute-start.6) | collective-permute-done | bytes 12320 | tf_op jit(solution)/shard_map/ppermute | solution.py:359
  19.4 0.9 %shard_map.91 = (bf16[2,384,128]{2,1,0:T(8,128)(2,1)S(1)}, bf16[2,384,128]{2,1,0:T(8,128)(2,1)S(1)}, bf16[768,384]{1,0:T(8,128)(2,1)S(1)}, bf16[384,384]{1,0:T(8,128)(2,1)S(1)}, f32[8,384]{1,0:T(8,128)S(1)}) custom-call(bf16[2,384,128]{2,1,0:T(8,128)(2,1)S(1)} %get-tuple-element.34.qg, f32[384,384]{1,0:T(8,128)S(1)} %get-tuple-element.38.s_early, ...), custom_call_target="tpu_custom_call" | custom-call | tf_op jit(solution)/shard_map/pallas_call | solution.py:402
  20.2 1.6 %collective-permute-start.7 = (bf16[2,384,128]{2,1,0:T(8,128)(2,1)S(1)}, bf16[2,384,128]{2,1,0:T(8,128)(2,1)S(1)}, u32[]{:S(2)}, u32[]{:S(2)}) collective-permute-start(bf16[2,384,128]{2,1,0:T(8,128)(2,1)S(1)} %get-tuple-element.50), channel_id=1, source_target_pairs={{0,2},{2,0},{4,6},{6,4},{8,10},{10,8},{12,14},{14,12},{16,18},{18,... | collective-permute-start | bytes 589832 | tf_op jit(solution)/shard_map/ppermute | solution.py:359
  21.8 0.9 %shard_map.92 = (bf16[2,384,128]{2,1,0:T(8,128)(2,1)S(1)}, f32[384,128]{1,0:T(8,128)S(1)}, bf16[192,128]{1,0:T(8,128)(2,1)S(1)}) custom-call(bf16[2,384,128]{2,1,0:T(8,128)(2,1)S(1)} %get-tuple-element.34.qg, f32[384,384]{1,0:T(8,128)S(1)} %get-tuple-element.35.s_own, f32[384,384]{1,0:T(8,128)S(1)} %get-tuple-element.36.d_own, ...), custom_call_target="tpu_custom_call" | custom-call | tf_op jit(solution)/shard_map/pallas_call | solution.py:408
  22.7 0.6 %collective-permute-start.9 = (bf16[192,128]{1,0:T(8,128)(2,1)S(1)}, bf16[192,128]{1,0:T(8,128)(2,1)S(1)}, u32[]{:S(2)}, u32[]{:S(2)}) collective-permute-start(bf16[192,128]{1,0:T(8,128)(2,1)S(1)} %get-tuple-element.53), channel_id=1, source_target_pairs={{0,16},{2,18},{4,20},{6,22},{8,24},{10,26},{12,28},{14,30},{16,0},... | collective-permute-start | bytes 147464 | tf_op jit(solution)/shard_map/ppermute | solution.py:359
  23.3 3.7 %collective-permute-done.9.refs_0_ = bf16[192,128]{1,0:T(8,128)(2,1)S(1)} collective-permute-done((bf16[192,128]{1,0:T(8,128)(2,1)S(1)}, bf16[192,128]{1,0:T(8,128)(2,1)S(1)}, u32[]{:S(2)}, u32[]{:S(2)}) %collective-permute-start.9) | collective-permute-done | bytes 49184 | tf_op jit(solution)/shard_map/ppermute | solution.py:359
  26.9 0.1 shard_map.93
  27.1 0.1 collective-permute-start.10
  27.1 1.4 %collective-permute-done.10.swap_ref = bf16[3,192,128]{2,1,0:T(8,128)(2,1)S(1)} collective-permute-done((bf16[3,192,128]{2,1,0:T(8,128)(2,1)S(1)}, bf16[3,192,128]{2,1,0:T(8,128)(2,1)S(1)}, u32[]{:S(2)}, u32[]{:S(2)}) %collective-permute-start.10) | collective-permute-done | bytes 147488 | tf_op jit(solution)/shard_map/ppermute | solution.py:362
  28.5 0.7 %shard_map.94 = (bf16[1,1,2,1,192,128]{5,4,3,2,1,0:T(8,128)(2,1)}, bf16[1,1,2,1,192,128]{5,4,3,2,1,0:T(8,128)(2,1)}, bf16[1,1,2,1,192,128]{5,4,3,2,1,0:T(8,128)(2,1)}) custom-call(bf16[2,192,128]{2,1,0:T(8,128)(2,1)S(1)} %get-tuple-element.54.mine_ref, bf16[3,192,128]{2,1,0:T(8,128)(2,1)S(1)} %collective-permute-done.10.swap_ref, ...), custom_call_target="tpu_custom_call" | custom-call | tf_op jit(solution)/shard_map/pallas_call | solution.py:419
  (8 shorter events, 0.1 us)
Async XLA Ops:
  1.8 1.7 %collective-permute-start = (bf16[976,128]{1,0:T(8,128)(2,1)S(1)}, bf16[976,128]{1,0:T(8,128)(2,1)S(1)}, u32[]{:S(2)}, u32[]{:S(2)}) collective-permute-start(bf16[976,128]{1,0:T(8,128)(2,1)S(1)} %get-tuple-element.32), channel_id=1, source_target_pairs={{0,8},{8,0},{16,24},{24,16},{1,9},{9,1},{17,25},{25,17},{2,10},{10... | collective-permute-start | bytes 749576 | tf_op jit(solution)/shard_map/ppermute | solution.py:362
  3.5 11.3 %collective-permute-start.5 = (bf16[400,128]{1,0:T(8,128)(2,1)S(1)}, bf16[400,128]{1,0:T(8,128)(2,1)S(1)}, u32[]{:S(2)}, u32[]{:S(2)}) collective-permute-start(bf16[400,128]{1,0:T(8,128)(2,1)S(1)} %get-tuple-element.39), channel_id=1, source_target_pairs={{0,16},{2,18},{4,20},{6,22},{8,24},{10,26},{12,28},{14,30},{16,0},... | collective-permute-start | bytes 307208 | tf_op jit(solution)/shard_map/ppermute | solution.py:359
  6.4 5.1 %collective-permute-start.2 = (bf16[2,192,128]{2,1,0:T(8,128)(2,1)S(1)}, bf16[2,192,128]{2,1,0:T(8,128)(2,1)S(1)}, u32[]{:S(2)}, u32[]{:S(2)}) collective-permute-start(bf16[2,192,128]{2,1,0:T(8,128)(2,1)S(1)} %get-tuple-element.30.kv_ref.refs_0_), channel_id=1, source_target_pairs={{0,8},{2,4},{4,2},{6,14},{8,0},{10,12},{12,10},{14,6},{16,24},{18,... | collective-permute-start | bytes 294920 | tf_op jit(solution)/shard_map/ppermute | solution.py:359
  6.4 5.8 %collective-permute-start.1 = (bf16[2,192,128]{2,1,0:T(8,128)(2,1)S(1)}, bf16[2,192,128]{2,1,0:T(8,128)(2,1)S(1)}, u32[]{:S(2)}, u32[]{:S(2)}) collective-permute-start(bf16[2,192,128]{2,1,0:T(8,128)(2,1)S(1)} %get-tuple-element.30.kv_ref.refs_0_), channel_id=1, source_target_pairs={{0,2},{2,0},{4,6},{6,4},{8,10},{10,8},{12,14},{14,12},{16,18},{18,... | collective-permute-start | bytes 294920 | tf_op jit(solution)/shard_map/ppermute | solution.py:359
  9.6 3.0 %collective-permute-start.4 = (bf16[2,192,128]{2,1,0:T(8,128)(2,1)S(1)}, bf16[2,192,128]{2,1,0:T(8,128)(2,1)S(1)}, u32[]{:S(2)}, u32[]{:S(2)}) collective-permute-start(bf16[2,192,128]{2,1,0:T(8,128)(2,1)S(1)} %get-tuple-element.33.par_kv_ref.refs_1_), channel_id=1, source_target_pairs={{0,8},{2,4},{4,2},{6,14},{8,0},{10,12},{12,10},{14,6},{16,24},{18,... | collective-permute-start | bytes 294920 | tf_op jit(solution)/shard_map/ppermute | solution.py:359
  9.6 5.2 %collective-permute-start.3 = (bf16[2,192,128]{2,1,0:T(8,128)(2,1)S(1)}, bf16[2,192,128]{2,1,0:T(8,128)(2,1)S(1)}, u32[]{:S(2)}, u32[]{:S(2)}) collective-permute-start(bf16[2,192,128]{2,1,0:T(8,128)(2,1)S(1)} %get-tuple-element.33.par_kv_ref.refs_1_), channel_id=1, source_target_pairs={{0,2},{2,0},{4,6},{6,4},{8,10},{10,8},{12,14},{14,12},{16,18},{18,... | collective-permute-start | bytes 294920 | tf_op jit(solution)/shard_map/ppermute | solution.py:359
  15.6 3.8 %collective-permute-start.6 = (f32[8,384]{1,0:T(8,128)S(1)}, f32[8,384]{1,0:T(8,128)S(1)}, u32[]{:S(2)}, u32[]{:S(2)}) collective-permute-start(f32[8,384]{1,0:T(8,128)S(1)} %get-tuple-element.45.refs_0_), channel_id=1, source_target_pairs={{0,16},{2,18},{4,20},{6,22},{8,24},{10,26},{12,28},{14,30},{16,0},... | collective-permute-start | bytes 36872 | tf_op jit(solution)/shard_map/ppermute | solution.py:359
  20.2 6.7 %collective-permute-start.7 = (bf16[2,384,128]{2,1,0:T(8,128)(2,1)S(1)}, bf16[2,384,128]{2,1,0:T(8,128)(2,1)S(1)}, u32[]{:S(2)}, u32[]{:S(2)}) collective-permute-start(bf16[2,384,128]{2,1,0:T(8,128)(2,1)S(1)} %get-tuple-element.50), channel_id=1, source_target_pairs={{0,2},{2,0},{4,6},{6,4},{8,10},{10,8},{12,14},{14,12},{16,18},{18,... | collective-permute-start | bytes 589832 | tf_op jit(solution)/shard_map/ppermute | solution.py:359
  21.8 5.1 %collective-permute-start.8 = (bf16[2,384,128]{2,1,0:T(8,128)(2,1)S(1)}, bf16[2,384,128]{2,1,0:T(8,128)(2,1)S(1)}, u32[]{:S(2)}, u32[]{:S(2)}) collective-permute-start(bf16[2,384,128]{2,1,0:T(8,128)(2,1)S(1)} %get-tuple-element.51), channel_id=1, source_target_pairs={{0,8},{2,4},{4,2},{6,14},{8,0},{10,12},{12,10},{14,6},{16,24},{18,... | collective-permute-start | bytes 589832 | tf_op jit(solution)/shard_map/ppermute | solution.py:359
  22.7 4.2 %collective-permute-start.9 = (bf16[192,128]{1,0:T(8,128)(2,1)S(1)}, bf16[192,128]{1,0:T(8,128)(2,1)S(1)}, u32[]{:S(2)}, u32[]{:S(2)}) collective-permute-start(bf16[192,128]{1,0:T(8,128)(2,1)S(1)} %get-tuple-element.53), channel_id=1, source_target_pairs={{0,16},{2,18},{4,20},{6,22},{8,24},{10,26},{12,28},{14,30},{16,0},... | collective-permute-start | bytes 147464 | tf_op jit(solution)/shard_map/ppermute | solution.py:359
  27.1 1.4 %collective-permute-start.10 = (bf16[3,192,128]{2,1,0:T(8,128)(2,1)S(1)}, bf16[3,192,128]{2,1,0:T(8,128)(2,1)S(1)}, u32[]{:S(2)}, u32[]{:S(2)}) collective-permute-start(bf16[3,192,128]{2,1,0:T(8,128)(2,1)S(1)} %get-tuple-element.55), channel_id=1, source_target_pairs={{0,8},{8,0},{16,24},{24,16},{1,9},{9,1},{17,25},{25,17},{2,10},{10... | collective-permute-start | bytes 442376 | tf_op jit(solution)/shard_map/ppermute | solution.py:362

commit v3 on v2

v3 whole, which is shorter than its diff:
```python
import functools

import jax
import jax.numpy as jnp
from jax import lax
from jax.experimental import pallas as pl
from jax.experimental.pallas import tpu as pltpu
from jax.sharding import PartitionSpec as P

VMEM = pl.BlockSpec(memory_space=pltpu.VMEM)
HBM = pl.BlockSpec(memory_space=pltpu.HBM)
LIMIT = pltpu.CompilerParams(vmem_limit_bytes=32 * 1024 * 1024)
ROWS_T = (((1,), (1,)), ((), ()))
COLS_T = (((0,), (0,)), ((), ()))


def dot(a, b, dims=(((1,), (0,)), ((), ()))):
    return lax.dot_general(a, b, dims, preferred_element_type=jnp.float32)


def place():
    t = lax.axis_index("tm")
    return t // 2, t % 2, lax.axis_index("height")


def pair(index, which):
    rising = (index % 2) == (0 if which == 0 else 1)
    return rising, jnp.where(rising, index + 1, index - 1)


def within(index, size):
    return (index >= 0) & (index < size)


def pack_kernel(tok, k_ref, v_ref, q_ref, g_ref, o_ref, mask_ref, kv_ref, rest_ref, other_ref, flags, sems):
    _, c, _ = place()
    copies = [pltpu.make_async_copy(mask_ref, flags, sems.at[10])]
    for i, ref in enumerate((k_ref, v_ref, q_ref, g_ref, o_ref)):
        own = (kv_ref if i < 2 else rest_ref).at[pl.ds((i if i < 2 else i - 2) * tok, tok), :]
        copies.append(pltpu.make_async_copy(ref.at[0, 0, c, 0], own, sems.at[2 * i + 1]))
        copies.append(
            pltpu.make_async_copy(ref.at[0, 0, 1 - c, 0], other_ref.at[pl.ds(i * tok, tok), :], sems.at[2 * i])
        )
    for copy in copies:
        copy.start()
    copies[0].wait()
    row = lax.broadcasted_iota(jnp.int32, (16, rest_ref.shape[1]), 0)
    spread = jnp.zeros(row.shape, jnp.float32)
    for i in range(9):
        on = (flags[0, 0, 0, 9 * (i // 3) + 3 * (i % 3) + 1] != 0).astype(jnp.float32)
        spread = jnp.where(row == i, on, spread)
    rest_ref[pl.ds(3 * tok, 16), :] = spread.astype(jnp.bfloat16)
    other_ref[pl.ds(5 * tok, 16), :] = spread.astype(jnp.bfloat16)
    for copy in copies[1:]:
        copy.wait()


def rows_at(index, tok):
    return pl.ds(index * tok, tok)


def border_is_own(y, c):
    rising, _ = pair(y, 0)
    return (c == 1) == rising


def pick(near, which, own, par):
    return jnp.where(near, own, par) if which == 0 else jnp.where(near, par, own)


def line_kernel(tok, rest_ref, par_ref, par_kv_ref, *border_refs):
    y, c, _ = place()
    near = border_is_own(y, c)
    for i in range(2):
        par_kv_ref[rows_at(i, tok), :] = par_ref[rows_at(i, tok), :]
    width = par_ref.shape[1]
    f32 = jnp.float32
    for which, ref in enumerate(border_refs):
        tiles = [pick(near, which, rest_ref[rows_at(i, tok), :], par_ref[rows_at(i + 2, tok), :]) for i in range(3)]
        ref[rows_at(0, tok), :], ref[rows_at(1, tok), :] = tiles[0], tiles[1]
        flags = pick(near, which, rest_ref[pl.ds(3 * tok, 16), :], par_ref[pl.ds(5 * tok, 16), :]).astype(f32)
        product, gap = tiles[1].astype(f32) * tiles[2].astype(f32), jnp.zeros((2 * width - tok, width), f32)
        product = jnp.concatenate([product, gap] if which == 0 else [gap, product], axis=0)
        left, lines = jnp.sum(product.T, axis=0, keepdims=True), [flags[0:9]]
        for _ in range(3):
            term = left.astype(jnp.bfloat16).astype(f32)
            left = left - term
            lines += [term[:, :width], term[:, width:]]
        ref[pl.ds(2 * tok, 16), :] = jnp.concatenate(lines + [jnp.zeros((1, width), f32)], axis=0).astype(jnp.bfloat16)


def foreign_delta(ref, which, tok):
    terms = ref[pl.ds(2 * tok, 16), :].astype(jnp.float32)
    one, two = (sum(terms[9 + 2 * i + half : 10 + 2 * i + half] for i in range(3)) for half in range(2))
    none = jnp.zeros_like(one)
    return jnp.concatenate([one, two, none] if which == 0 else [none, one, two], axis=1)


def line_place(z, line, heights):
    if line == 0:
        return True, lambda flags, dt: flags[3 * dt + 1 : 3 * dt + 2]
    rising, at = pair(z, line - 1)
    return within(at, heights), lambda flags, dt: jnp.where(
        rising, flags[3 * dt + 2 : 3 * dt + 3], flags[3 * dt : 3 * dt + 1]
    )


def lanes_of(tok, border, other):
    width = border.shape[1]
    lane = lax.broadcasted_iota(jnp.int32, (1, width), 1)
    return jnp.concatenate(
        [jnp.where(lane + start < tok, border, other) for start in range(0, 2 * tok, width)], axis=1
    )


def first_kernel(tok, heights, scale, kv_ref, par_kv_ref, rest_ref, par_ref, qg, table, s_ref, d_ref):
    y, c, z = place()
    two = 2 * tok
    f32 = jnp.float32
    first, near = c == 0, border_is_own(y, c)
    out = []
    for part in range(3):
        own, par = rest_ref[rows_at(part, tok), :], par_ref[rows_at(part + 2, tok), :]
        tiles = [pick(near, which, own, par) for which in range(2)]
        if part == 2:
            out = jnp.concatenate(tiles, axis=0)
        else:
            for which in range(2):
                qg[part, rows_at(which, tok), :] = tiles[which]
    delta = jnp.sum((qg[1].astype(f32) * out.astype(f32)).T, axis=0, keepdims=True)

    own_flags = rest_ref[pl.ds(3 * tok, 16), :].astype(f32)
    par_flags = par_ref[pl.ds(5 * tok, 16), :].astype(f32)
    lines = []
    for line in range(3):
        inside, at = line_place(z, line, heights)
        centre = jnp.ones_like(own_flags[0:1]) if line == 0 else None
        for slot in range(2):
            if slot == 0:
                own, par = at(own_flags, 1), jnp.where(first, at(par_flags, 0), at(par_flags, 2))
            else:
                own, par = jnp.where(first, at(own_flags, 2), at(own_flags, 0)), at(par_flags, 1)
            if line == 0:
                own, par = (centre, par) if slot == 0 else (own, centre)
            row = lanes_of(tok, pick(near, 0, own, par), pick(near, 1, own, par))
            lines.append(jnp.where(inside, (row - 1.0) * 1e30, -1e30))
    table[...] = jnp.concatenate(lines + [delta, jnp.zeros((1, two), f32)], axis=0)
    for i, source in enumerate((kv_ref, par_kv_ref)):
        rows = rows_at(i, tok)
        s_ref[rows, :] = dot(source[rows_at(0, tok), :], qg[0], ROWS_T) * scale + table[i : i + 1, :]
        d_ref[rows, :] = dot(source[rows_at(1, tok), :], qg[1], ROWS_T) - table[6:7, :]


def largest(tok, blocks):
    top = jnp.full((8, 2 * tok), -1e30, jnp.float32)
    for ref, i in blocks:
        top = jnp.maximum(top, jnp.max(ref[rows_at(i, tok), :].reshape(tok // 8, 8, 2 * tok), axis=0))
    return jnp.max(top, axis=0, keepdims=True)


def summed(tok, blocks, top):
    total = jnp.zeros((8, 2 * tok), jnp.float32)
    for ref, i in blocks:
        weights = jnp.exp(ref[rows_at(i, tok), :] - top)
        total = total + jnp.sum(weights.reshape(tok // 8, 8, 2 * tok), axis=0)
    return jnp.sum(total, axis=0, keepdims=True)


def early_kernel(tok, scale, qg, table, s_own, one_ref, two_ref, s_ref, d_ref, part_ref):
    for i, source in enumerate((one_ref, two_ref)):
        rows = rows_at(i, tok)
        s_ref[rows, :] = dot(source[rows_at(0, tok), :], qg[0], ROWS_T) * scale + table[2 + 2 * i : 3 + 2 * i, :]
        d_ref[rows, :] = dot(source[rows_at(1, tok), :], qg[1], ROWS_T) - table[6:7, :]
    blocks = [(ref, i) for ref in (s_own, s_ref) for i in range(2)]
    top = largest(tok, blocks)
    total = summed(tok, blocks, top)
    part_ref[...] = jnp.concatenate([top, total, jnp.zeros((6, 2 * tok), jnp.float32)], axis=0)


def foreign_rows(ref, part, which, tok):
    block = ref[rows_at(part, tok), :]
    return jnp.concatenate([block, jnp.zeros_like(block)] if which == 0 else [jnp.zeros_like(block), block], axis=0)


def score_kernel(tok, chips, heights, sides, scale, qg, table, part, *refs):
    keys, foreign, refs = refs[:6], refs[6 : 6 + sides], refs[6 + sides :]
    s_late, s_far, *notes = refs
    y, c, z = place()
    near = border_is_own(y, c)
    two = 2 * tok
    f32 = jnp.float32
    far = []
    for which in range(sides):
        rising, y_at = pair(y, which)
        flags = foreign[which][pl.ds(2 * tok, 16), :].astype(f32)
        queries = foreign_rows(foreign[which], 0, which, tok)
        for line in range(3):
            inside, at = line_place(z, line, heights)
            row = jnp.where(rising, at(flags, 0), at(flags, 2))
            none = jnp.zeros_like(row)
            row = lanes_of(tok, *((row, none) if which == 0 else (none, row)))
            bias = jnp.where(inside & within(y_at, chips), (row - 1.0) * 1e30, -1e30)
            border = pick(near, which, keys[2 * line][rows_at(0, tok), :], keys[2 * line + 1][rows_at(0, tok), :])
            s_far[rows_at(3 * which + line, tok), :] = dot(border, queries, ROWS_T) * scale + bias
        blocks = [(s_far, 3 * which + line) for line in range(3)]
        top = largest(tok, blocks)
        far.append([top, summed(tok, blocks, top)])
    for i in range(2):
        scores = dot(keys[3 + 2 * i][rows_at(0, tok), :], qg[0], ROWS_T) * scale
        s_late[rows_at(i, tok), :] = scores + table[3 + 2 * i : 4 + 2 * i, :]
    blocks = [(s_late, i) for i in range(2)]
    top = jnp.maximum(part[0:1, :], largest(tok, blocks))
    total = part[1:2, :] * jnp.exp(part[0:1, :] - top) + summed(tok, blocks, top)
    for which in range(sides):
        notes[which][...] = jnp.concatenate([top, total] + far[which] + [jnp.zeros((4, two), f32)], axis=0)


def middle_kernel(tok, sides, scale, qg, table, s_own, d_own, s_early, d_early, s_late, s_far, *refs):
    tiles, foreign, sent = refs[:6], refs[6 : 6 + sides], refs[6 + sides : 6 + 2 * sides]
    e_ref, ds_ref, e_far, ds_far, dq_ref, *far_dq = refs[6 + 2 * sides :]
    y, c, _ = place()
    near = border_is_own(y, c)
    f32, bf16 = jnp.float32, jnp.bfloat16
    dq = jnp.zeros(dq_ref.shape, f32)
    for line, scores in enumerate(((s_own, s_own), (s_early, s_late), (s_early, s_late))):
        for slot in range(2):
            i, at = 2 * line + slot, rows_at(max(line - 1, 0) if line else slot, tok)
            weights = jnp.exp(scores[slot][at, :] - sent[0][0:1, :])
            if line and slot:
                grads = dot(tiles[i][rows_at(1, tok), :], qg[1], ROWS_T) - table[6:7, :]
            else:
                grads = (d_early if line else d_own)[at, :]
            low = (weights * grads * scale).astype(bf16)
            e_ref[rows_at(i, tok), :] = weights.astype(bf16)
            ds_ref[rows_at(i, tok), :] = low
            dq = dq + dot(tiles[i][rows_at(0, tok), :], low, COLS_T)
    dq_ref[...] = dq
    for which in range(sides):
        far_g = foreign_rows(foreign[which], 1, which, tok)
        delta = foreign_delta(foreign[which], which, tok)
        dq = jnp.zeros(dq_ref.shape, f32)
        for line in range(3):
            rows = rows_at(3 * which + line, tok)
            own, par = tiles[2 * line], tiles[2 * line + 1]
            key, value = (pick(near, which, own[rows_at(i, tok), :], par[rows_at(i, tok), :]) for i in range(2))
            weights = jnp.exp(s_far[rows, :] - sent[which][2:3, :])
            low = (weights * (dot(value, far_g, ROWS_T) - delta) * scale).astype(bf16)
            e_far[rows, :] = weights.astype(bf16)
            ds_far[rows, :] = low
            dq = dq + dot(key, low, COLS_T)
        far_dq[which][...] = dq


def column_sums(tok, near, sides, line, slot, e_ref, ds_ref, e_far, ds_far, scaled, far_scaled):
    rows = rows_at(2 * line + slot, tok)
    sums = [dot(ds_ref[rows, :], scaled[0]), dot(e_ref[rows, :], scaled[1])]
    for which in range(sides):
        rows = rows_at(3 * which + line, tok)
        mine = near == ((slot == 0) == (which == 0))
        for i, ref in enumerate((ds_far, e_far)):
            sums[i] = sums[i] + jnp.where(mine, dot(ref[rows, :], far_scaled[which][i]), 0.0)
    return [part.astype(jnp.bfloat16) for part in sums]


def leave_kernel(tok, chips, sides, qg, e_ref, ds_ref, e_far, ds_far, *refs):
    far_dq, sent, came, foreign = (refs[i * sides : (i + 1) * sides] for i in range(4))
    one_ref, two_ref, scaled, factor_ref, *refs = refs[4 * sides :]
    shares, far_scaled = refs[:sides], refs[sides:]
    y, c, _ = place()
    near = border_is_own(y, c)
    bf16 = jnp.bfloat16
    width = qg.shape[2]

    def log_total(top, total, other_top, other_total):
        both = jnp.maximum(top, other_top)
        return both + jnp.log(total * jnp.exp(top - both) + other_total * jnp.exp(other_top - both))

    def times(block, factor):
        return (block.astype(jnp.float32) * jnp.broadcast_to(factor, (width, 2 * tok)).T).astype(bf16)

    top, total = sent[0][0:1, :], sent[0][1:2, :]
    lse = None
    for which in range(sides):
        _, y_at = pair(y, which)
        inside = within(y_at, chips)
        note = came[which]
        far_lse = log_total(note[0:1, :], note[1:2, :], sent[which][2:3, :], sent[which][3:4, :])
        factor = jnp.where(inside, jnp.exp(sent[which][2:3, :] - far_lse), 0.0)
        share = (far_dq[which][...] * factor).T
        shares[which][...] = share[which * tok : (which + 1) * tok].astype(bf16)
        for part in range(2):
            far_scaled[which][part] = times(foreign_rows(foreign[which], part, which, tok), factor)
        other = jnp.where(inside, note[2:3, :], -1e30), jnp.where(inside, note[3:4, :], 0.0)
        lse = log_total(top, total, *other) if which == 0 else log_total(lse, jnp.ones_like(lse), *other)
    factor = jnp.exp(top - lse)
    factor_ref[...] = jnp.broadcast_to(factor, factor_ref.shape)
    for part in range(2):
        scaled[part] = times(qg[part], factor)
    for line, result in ((1, one_ref), (2, two_ref)):
        for slot in range(2):
            sums = column_sums(tok, near, sides, line, slot, e_ref, ds_ref, e_far, ds_far, scaled, far_scaled)
            for i in range(2):
                result[i, rows_at(slot, tok), :] = sums[i]


def stay_kernel(tok, sides, e_ref, ds_ref, e_far, ds_far, scaled, factor_ref, raw_dq, *refs):
    far_scaled, (own_ref, dq_ref) = refs[:sides], refs[sides:]
    y, c, _ = place()
    near = border_is_own(y, c)
    for slot in range(2):
        sums = column_sums(tok, near, sides, 0, slot, e_ref, ds_ref, e_far, ds_far, scaled, far_scaled)
        for i in range(2):
            own_ref[i, rows_at(slot, tok), :] = sums[i]
    dq_ref[...] = (raw_dq[...] * factor_ref[0:1, :]).T


def sum_kernel(tok, chips, heights, sides, own_ref, one_ref, two_ref, dq_ref, *refs):
    backs, (mine_ref, mine_q_ref, swap_ref) = refs[:sides], refs[sides:]
    y, c, z = place()
    near = border_is_own(y, c)
    f32, bf16 = jnp.float32, jnp.bfloat16
    for i in range(2):
        for slot in range(2):
            rows = rows_at(slot, tok)
            value = own_ref[i, rows, :].astype(f32)
            for line, ref in ((1, one_ref), (2, two_ref)):
                inside, _ = line_place(z, line, heights)
                value = value + jnp.where(inside, ref[i, rows, :].astype(f32), 0.0)
            if slot == 0:
                mine_ref[i] = value.astype(bf16)
            else:
                swap_ref[i] = value.astype(bf16)
    tiles = []
    for tile in range(2):
        value = dq_ref[rows_at(tile, tok), :]
        if tile < sides:
            _, y_at = pair(y, tile)
            value = value + jnp.where(within(y_at, chips), backs[tile][...].astype(f32), 0.0)
        tiles.append(value.astype(bf16))
    mine_q_ref[...] = jnp.where(near, tiles[0], tiles[1])
    swap_ref[2] = jnp.where(near, tiles[1], tiles[0])


def final_kernel(mine_ref, swap_ref, mine_q_ref, gq_ref, gk_ref, gv_ref):
    _, c, _ = place()
    gq_ref[0, 0, c, 0] = mine_q_ref[...]
    gq_ref[0, 0, 1 - c, 0] = swap_ref[2]
    for i, ref in enumerate((gk_ref, gv_ref)):
        ref[0, 0, c, 0] = mine_ref[i]
        ref[0, 0, 1 - c, 0] = swap_ref[i]


def body(queries, keys, values, grad_out, attn_out, window_mask):
    tok, width = queries.shape[-2:]
    scale = width ** -0.5
    times, heights = lax.axis_size("tm"), lax.axis_size("height")
    chips = times // 2
    sides = 1 if chips == 2 else 2
    bf16, f32 = jnp.bfloat16, jnp.float32

    def call(kernel, shapes, specs, scratch=()):
        return pl.pallas_call(
            kernel,
            out_shape=[jax.ShapeDtypeStruct(*shape) for shape in shapes],
            in_specs=list(specs),
            out_specs=[VMEM] * len(shapes),
            scratch_shapes=list(scratch),
            compiler_params=LIMIT,
        )

    def partner(index, which, size):
        if which is None:
            return index
        at = index + 1 if index % 2 == which else index - 1
        return at if 0 <= at < size else None

    def exchange(block, y_which, z_which):
        pairs = []
        for t in range(times):
            for z in range(heights):
                y_at, z_at = partner(t // 2, y_which, chips), partner(z, z_which, heights)
                at = t * heights + z
                alone = y_at is None or z_at is None
                pairs.append((at, (t ^ 1) * heights + z if alone else (2 * y_at + t % 2) * heights + z_at))
        return lax.ppermute(block, ("tm", "height"), pairs)

    def swap_cores(block):
        return lax.ppermute(block, "tm", [(t, t ^ 1) for t in range(times)])

    line_shape, tile_shape = ((2, 2 * tok, width), bf16), ((2, tok, width), bf16)
    extra = 32
    arguments = (keys, values, queries, grad_out, attn_out, window_mask)
    kv, rest, other = call(
        functools.partial(pack_kernel, tok),
        [((2 * tok + extra, width), bf16), ((3 * tok + 16, width), bf16), ((5 * tok + 16, width), bf16)],
        [HBM] * 6,
        [pltpu.SMEM(window_mask.shape, jnp.int32), pltpu.SemaphoreType.DMA((11,))],
    )(*(pltpu.with_memory_space_constraint(x, pltpu.HBM) for x in arguments))
    early = [exchange(kv, None, which) for which in range(2)]
    par = swap_cores(other)
    border_shape, two = ((2 * tok + 16, width), bf16), 2 * tok
    par_kv, *borders = call(
        functools.partial(line_kernel, tok), [((2 * tok, width), bf16)] + [border_shape] * sides, [VMEM] * 2
    )(rest, par)
    foreign = [exchange(borders[which], which, None) for which in range(sides)]
    late = [exchange(par_kv, None, which) for which in range(2)]
    tiles = (kv, par_kv, early[0], late[0], early[1], late[1])
    pair_shape, note_shape, raw_shape = ((2, two, width), bf16), ((8, two), f32), ((width, two), f32)

    def square(count, kind=f32):
        return ((count * tok, two), kind)

    qg, table, s_own, d_own = call(
        functools.partial(first_kernel, tok, heights, scale),
        [pair_shape, note_shape, square(2), square(2)],
        [VMEM] * 4,
    )(kv, par_kv, rest, par)
    s_early, d_early, part = call(
        functools.partial(early_kernel, tok, scale), [square(2), square(2), note_shape], [VMEM] * 5
    )(qg, table, s_own, *early)
    s_late, s_far, *sent = call(
        functools.partial(score_kernel, tok, chips, heights, sides, scale),
        [square(2), square(3 * sides)] + [note_shape] * sides,
        [VMEM] * (9 + sides),
    )(qg, table, part, *tiles, *foreign)
    came = [exchange(sent[which], which, None) for which in range(sides)]
    e, ds, e_far, ds_far, raw_dq, *far_dq = call(
        functools.partial(middle_kernel, tok, sides, scale),
        [square(6, bf16)] * 2 + [square(3 * sides, bf16)] * 2 + [raw_shape] * (1 + sides),
        [VMEM] * (14 + 2 * sides),
    )(qg, table, s_own, d_own, s_early, d_early, s_late, s_far, *tiles, *foreign, *sent)
    one, other_one, scaled, factor, *rest_out = call(
        functools.partial(leave_kernel, tok, chips, sides),
        [line_shape, line_shape, pair_shape, note_shape] + [((tok, width), bf16)] * sides + [pair_shape] * sides,
        [VMEM] * (5 + 4 * sides),
    )(qg, e, ds, e_far, ds_far, *far_dq, *sent, *came, *foreign)
    shares, far_scaled = rest_out[:sides], rest_out[sides:]
    back = [exchange(block, None, which) for which, block in enumerate((one, other_one))]
    shares = [exchange(share, which, None) for which, share in enumerate(shares)]
    own, dq = call(
        functools.partial(stay_kernel, tok, sides),
        [line_shape, ((two, width), f32)],
        [VMEM] * (7 + sides),
    )(e, ds, e_far, ds_far, scaled, factor, raw_dq, *far_scaled)
    mine, mine_q, leaving = call(
        functools.partial(sum_kernel, tok, chips, heights, sides),
        [tile_shape, ((tok, width), bf16), ((3, tok, width), bf16)],
        [VMEM] * (4 + sides),
    )(own, *back, dq, *shares)
    return call(final_kernel, [(queries.shape, bf16)] * 3, [VMEM] * 3)(mine, swap_cores(leaving), mine_q)


def solution(mesh):
    placed = P("tm", "height", "dp", None, None, None)
    return jax.shard_map(
        body,
        mesh=mesh,
        in_specs=(placed,) * 5 + (P("tm", "height", None, None),),
        out_specs=(placed,) * 3,
        check_vma=False,
    )
```

time: 29.4 us -> 27 us (0.918)
  waiting for transfers between devices: 11.9 us -> 8.78 us
  Pallas kernels: 5.65 us -> 6.38 us
    ppermute x9, waiting for transfers between devices: 9.38 us -> 7.42 us  [exchange(): return lax.ppermute(block, ('tm', 'height'), pairs)]
    ppermute x2, waiting for transfers between devices: 2.5 us -> 1.36 us  [swap_cores(): return lax.ppermute(block, 'tm', [(t, t ^ 1) for t in range(times)])]
    pallas_call x7, Pallas kernels: 3.96 us -> 4.91 us  [the longest x1 1.34 us: body(): call(functools.partial(middle_kernel, tok, sides, scale), [square(6, bf16...]
  transfers between devices with their start and end apart: 11 -> 11, of which waited for: 6 -> 5; matrix products, arithmetic and copies ran while one was open for 0% -> 0% of each run, Pallas kernels for 7% -> 10%
where the time goes in v3:
time: 27 us; the launch traced here: 26.9 us
  starting transfers between devices  11 us (41%)
  waiting for transfers between devices  8.78 us (33%)
  Pallas kernels  6.38 us (24%)
  between operations  0.72 us (3%)
    ppermute x9, starting transfers between devices, exchange(): return lax.ppermute(block, ('tm', 'height'), pairs)  10.4 us
    ppermute x9, waiting for transfers between devices, exchange(): return lax.ppermute(block, ('tm', 'height'), pairs)  7.42 us
    ppermute x2, waiting for transfers between devices, swap_cores(): return lax.ppermute(block, 'tm', [(t, t ^ 1) for t in range(times)])  1.36 us
    pallas_call x1, Pallas kernels, body(): call(functools.partial(middle_kernel, tok, sides, scale), [square(6, bf16...  1.34 us
    pallas_call x1, Pallas kernels, body(): call(functools.partial(pack_kernel, tok), [((2 * tok + extra, width), bf1...  1.12 us
    pallas_call x1, Pallas kernels, body(): call(functools.partial(leave_kernel, tok, chips, sides), [line_shape, lin...  0.97 us
    pallas_call x1, Pallas kernels, body(): call(final_kernel, [(queries.shape, bf16)] * 3, [VMEM] * 3)  0.74 us
    pallas_call x1, Pallas kernels, body(): call(functools.partial(score_kernel, tok, chips, heights, sides, scale),...  0.6 us
  transfers between devices with their start and end apart: 11, of which 5 were waited for; matrix products, arithmetic and copies ran while one was open for 0% of the time, Pallas kernels for 10%

profile of v3, /device:TPU:0, one launch (start us, length us, event | category | flops | bytes accessed | tf_op | source)
XLA Modules:
  0.0 26.9 jit_solution(11335119956122352804)
XLA Ops:
  0.6 1.1 %shard_map.85 = (bf16[416,128]{1,0:T(8,128)(2,1)S(1)}, bf16[592,128]{1,0:T(8,128)(2,1)S(1)}, bf16[976,128]{1,0:T(8,128)(2,1)S(1)}) custom-call(bf16[1,1,2,1,192,128]{5,4,3,2,1,0:T(8,128)(2,1)} %k_ref.1, bf16[1,1,2,1,192,128]{5,4,3,2,1,0:T(8,128)(2,1)} %v_ref.1, bf16[1,1,2,1,192,128]{5,4,3,2,1,0:T(8,128)(2,1)} %q_ref.1, ...), custom_call_target="tpu_custom_call" | custom-call | tf_op jit(solution)/shard_map/pallas_call | solution.py:393
  1.8 0.5 %collective-permute-start = (bf16[976,128]{1,0:T(8,128)(2,1)S(1)}, bf16[976,128]{1,0:T(8,128)(2,1)S(1)}, u32[]{:S(2)}, u32[]{:S(2)}) collective-permute-start(bf16[976,128]{1,0:T(8,128)(2,1)S(1)} %get-tuple-element.37), channel_id=1, source_target_pairs={{0,8},{8,0},{16,24},{24,16},{1,9},{9,1},{17,25},{25,17},{2,10},{10... | collective-permute-start | bytes 749576 | tf_op jit(solution)/shard_map/ppermute | solution.py:388
  2.3 0.1 collective-permute-start.2
  2.4 4.1 %collective-permute-start.1 = (bf16[416,128]{1,0:T(8,128)(2,1)S(1)}, bf16[416,128]{1,0:T(8,128)(2,1)S(1)}, u32[]{:S(2)}, u32[]{:S(2)}) collective-permute-start(bf16[416,128]{1,0:T(8,128)(2,1)S(1)} %get-tuple-element.35.kv_ref.refs_0_), channel_id=1, source_target_pairs={{0,2},{2,0},{4,6},{6,4},{8,10},{10,8},{12,14},{14,12},{16,18},{18,... | collective-permute-start | bytes 319496 | tf_op jit(solution)/shard_map/ppermute | solution.py:385
  6.5 0.1 shard_map.86
  6.7 1.6 %collective-permute-start.5 = (bf16[400,128]{1,0:T(8,128)(2,1)S(1)}, bf16[400,128]{1,0:T(8,128)(2,1)S(1)}, u32[]{:S(2)}, u32[]{:S(2)}) collective-permute-start(bf16[400,128]{1,0:T(8,128)(2,1)S(1)} %get-tuple-element.46), channel_id=1, source_target_pairs={{0,16},{2,18},{4,20},{6,22},{8,24},{10,26},{12,28},{14,30},{16,0},... | collective-permute-start | bytes 307208 | tf_op jit(solution)/shard_map/ppermute | solution.py:385
  8.2 2.0 %collective-permute-start.3 = (bf16[384,128]{1,0:T(8,128)(2,1)S(1)}, bf16[384,128]{1,0:T(8,128)(2,1)S(1)}, u32[]{:S(2)}, u32[]{:S(2)}) collective-permute-start(bf16[384,128]{1,0:T(8,128)(2,1)S(1)} %get-tuple-element.38.par_kv_ref.refs_1_), channel_id=1, source_target_pairs={{0,2},{2,0},{4,6},{6,4},{8,10},{10,8},{12,14},{14,12},{16,18},{18,... | collective-permute-start | bytes 294920 | tf_op jit(solution)/shard_map/ppermute | solution.py:385
  10.3 0.4 %shard_map.87 = (bf16[2,384,128]{2,1,0:T(8,128)(2,1)S(1)}, f32[8,384]{1,0:T(8,128)S(1)}, f32[384,384]{1,0:T(8,128)S(1)}, f32[384,384]{1,0:T(8,128)S(1)}) custom-call(bf16[416,128]{1,0:T(8,128)(2,1)S(1)} %get-tuple-element.35.kv_ref.refs_0_, bf16[384,128]{1,0:T(8,128)(2,1)S(1)} %get-tuple-element.38.par_kv_ref.refs_1_, ...), custom_call_target="tpu_custom_call" | custom-call | tf_op jit(solution)/shard_map/pallas_call | solution.py:413
  10.7 0.5 %shard_map.88 = (f32[384,384]{1,0:T(8,128)S(1)}, f32[384,384]{1,0:T(8,128)S(1)}, f32[8,384]{1,0:T(8,128)S(1)}) custom-call(bf16[2,384,128]{2,1,0:T(8,128)(2,1)S(1)} %get-tuple-element.39.qg, f32[8,384]{1,0:T(8,128)S(1)} %get-tuple-element.40.table, f32[384,384]{1,0:T(8,128)S(1)} %get-tuple-element.41.s_own, ...), custom_call_target="tpu_custom_call" | custom-call | tf_op jit(solution)/shard_map/pallas_call | solution.py:418
  11.2 2.3 %collective-permute-done.3.refs_3_ = bf16[384,128]{1,0:T(8,128)(2,1)S(1)} collective-permute-done((bf16[384,128]{1,0:T(8,128)(2,1)S(1)}, bf16[384,128]{1,0:T(8,128)(2,1)S(1)}, u32[]{:S(2)}, u32[]{:S(2)}) %collective-permute-start.3) | collective-permute-done | bytes 98336 | tf_op jit(solution)/shard_map/ppermute | solution.py:385
  13.5 0.6 %shard_map.89 = (f32[384,384]{1,0:T(8,128)S(1)}, f32[576,384]{1,0:T(8,128)S(1)}, f32[8,384]{1,0:T(8,128)S(1)}) custom-call(bf16[2,384,128]{2,1,0:T(8,128)(2,1)S(1)} %get-tuple-element.39.qg, f32[8,384]{1,0:T(8,128)S(1)} %get-tuple-element.40.table, f32[8,384]{1,0:T(8,128)S(1)} %get-tuple-element.45.part, ...), custom_call_target="tpu_custom_call" | custom-call | tf_op jit(solution)/shard_map/pallas_call | solution.py:421
  14.1 0.6 %collective-permute-start.6 = (f32[8,384]{1,0:T(8,128)S(1)}, f32[8,384]{1,0:T(8,128)S(1)}, u32[]{:S(2)}, u32[]{:S(2)}) collective-permute-start(f32[8,384]{1,0:T(8,128)S(1)} %get-tuple-element.49.refs_7_.refs_1_), channel_id=1, source_target_pairs={{0,16},{2,18},{4,20},{6,22},{8,24},{10,26},{12,28},{14,30},{16,0},... | collective-permute-start | bytes 36872 | tf_op jit(solution)/shard_map/ppermute | solution.py:385
  14.6 1.3 %shard_map.90 = (bf16[1152,384]{1,0:T(8,128)(2,1)S(1)}, bf16[1152,384]{1,0:T(8,128)(2,1)S(1)}, bf16[576,384]{1,0:T(8,128)(2,1)S(1)}, bf16[576,384]{1,0:T(8,128)(...) custom-call(bf16[2,384,128]{2,1,0:T(8,128)(2,1)S(1)} %get-tuple-element.39.qg, ...), custom_call_target="tpu_custom_call" | custom-call | tf_op jit(solution)/shard_map/pallas_call | solution.py:427
  16.0 1.8 %collective-permute-done.6.refs_2_ = f32[8,384]{1,0:T(8,128)S(1)} collective-permute-done((f32[8,384]{1,0:T(8,128)S(1)}, f32[8,384]{1,0:T(8,128)S(1)}, u32[]{:S(2)}, u32[]{:S(2)}) %collective-permute-start.6) | collective-permute-done | bytes 12320 | tf_op jit(solution)/shard_map/ppermute | solution.py:385
  17.8 1.0 %shard_map.91 = (bf16[2,384,128]{2,1,0:T(8,128)(2,1)S(1)}, bf16[2,384,128]{2,1,0:T(8,128)(2,1)S(1)}, bf16[2,384,128]{2,1,0:T(8,128)(2,1)S(1)}, f32[8,384]{1,0:T(...) custom-call(bf16[2,384,128]{2,1,0:T(8,128)(2,1)S(1)} %get-tuple-element.39.qg, ...), custom_call_target="tpu_custom_call" | custom-call | tf_op jit(solution)/shard_map/pallas_call | solution.py:432
  18.8 1.5 %collective-permute-start.7 = (bf16[2,384,128]{2,1,0:T(8,128)(2,1)S(1)}, bf16[2,384,128]{2,1,0:T(8,128)(2,1)S(1)}, u32[]{:S(2)}, u32[]{:S(2)}) collective-permute-start(bf16[2,384,128]{2,1,0:T(8,128)(2,1)S(1)} %get-tuple-element.60), channel_id=1, source_target_pairs={{0,2},{2,0},{4,6},{6,4},{8,10},{10,8},{12,14},{14,12},{16,18},{18,... | collective-permute-start | bytes 589832 | tf_op jit(solution)/shard_map/ppermute | solution.py:385
  20.3 0.5 %collective-permute-start.9 = (bf16[192,128]{1,0:T(8,128)(2,1)S(1)}, bf16[192,128]{1,0:T(8,128)(2,1)S(1)}, u32[]{:S(2)}, u32[]{:S(2)}) collective-permute-start(bf16[192,128]{1,0:T(8,128)(2,1)S(1)} %get-tuple-element.63), channel_id=1, source_target_pairs={{0,16},{2,18},{4,20},{6,22},{8,24},{10,26},{12,28},{14,30},{16,0},... | collective-permute-start | bytes 147464 | tf_op jit(solution)/shard_map/ppermute | solution.py:385
  20.8 0.5 %shard_map.92 = (bf16[2,384,128]{2,1,0:T(8,128)(2,1)S(1)}, f32[384,128]{1,0:T(8,128)S(1)}) custom-call(bf16[1152,384]{1,0:T(8,128)(2,1)S(1)} %get-tuple-element.50.e_ref, bf16[1152,384]{1,0:T(8,128)(2,1)S(1)} %get-tuple-element.51.ds_ref, bf16[576,384]{1,0:T(8,128)(2,1)S(1)} %get-tuple-element.52.e_far, bf16[576,384]{1,0:T(8,128)(2,1)S(1)} %get-tuple-element.53.ds_far, ...), custom_call_target="tpu_custom_call" | custom-call | tf_op jit(solution)/shard_map/pallas_call | solution.py:440
  21.3 3.2 %collective-permute-done.9.refs_0_ = bf16[192,128]{1,0:T(8,128)(2,1)S(1)} collective-permute-done((bf16[192,128]{1,0:T(8,128)(2,1)S(1)}, bf16[192,128]{1,0:T(8,128)(2,1)S(1)}, u32[]{:S(2)}, u32[]{:S(2)}) %collective-permute-start.9) | collective-permute-done | bytes 49184 | tf_op jit(solution)/shard_map/ppermute | solution.py:385
  24.4 0.1 collective-permute-done.7.one_ref
  24.5 0.1 shard_map.93
  24.7 0.1 collective-permute-start.10
  24.8 1.4 %collective-permute-done.10.swap_ref = bf16[3,192,128]{2,1,0:T(8,128)(2,1)S(1)} collective-permute-done((bf16[3,192,128]{2,1,0:T(8,128)(2,1)S(1)}, bf16[3,192,128]{2,1,0:T(8,128)(2,1)S(1)}, u32[]{:S(2)}, u32[]{:S(2)}) %collective-permute-start.10) | collective-permute-done | bytes 147488 | tf_op jit(solution)/shard_map/ppermute | solution.py:388
  26.1 0.7 %shard_map.94 = (bf16[1,1,2,1,192,128]{5,4,3,2,1,0:T(8,128)(2,1)}, bf16[1,1,2,1,192,128]{5,4,3,2,1,0:T(8,128)(2,1)}, bf16[1,1,2,1,192,128]{5,4,3,2,1,0:T(8,128)(2,1)}) custom-call(bf16[2,192,128]{2,1,0:T(8,128)(2,1)S(1)} %get-tuple-element.64.mine_ref, bf16[3,192,128]{2,1,0:T(8,128)(2,1)S(1)} %collective-permute-done.10.swap_ref, ...), custom_call_target="tpu_custom_call" | custom-call | tf_op jit(solution)/shard_map/pallas_call | solution.py:450
  (8 shorter events, 0.0 us)
Async XLA Ops:
  1.8 4.7 %collective-permute-start = (bf16[976,128]{1,0:T(8,128)(2,1)S(1)}, bf16[976,128]{1,0:T(8,128)(2,1)S(1)}, u32[]{:S(2)}, u32[]{:S(2)}) collective-permute-start(bf16[976,128]{1,0:T(8,128)(2,1)S(1)} %get-tuple-element.37), channel_id=1, source_target_pairs={{0,8},{8,0},{16,24},{24,16},{1,9},{9,1},{17,25},{25,17},{2,10},{10... | collective-permute-start | bytes 749576 | tf_op jit(solution)/shard_map/ppermute | solution.py:388
  2.3 8.4 %collective-permute-start.2 = (bf16[416,128]{1,0:T(8,128)(2,1)S(1)}, bf16[416,128]{1,0:T(8,128)(2,1)S(1)}, u32[]{:S(2)}, u32[]{:S(2)}) collective-permute-start(bf16[416,128]{1,0:T(8,128)(2,1)S(1)} %get-tuple-element.35.kv_ref.refs_0_), channel_id=1, source_target_pairs={{0,8},{2,4},{4,2},{6,14},{8,0},{10,12},{12,10},{14,6},{16,24},{18,... | collective-permute-start | bytes 319496 | tf_op jit(solution)/shard_map/ppermute | solution.py:385
  2.4 8.3 %collective-permute-start.1 = (bf16[416,128]{1,0:T(8,128)(2,1)S(1)}, bf16[416,128]{1,0:T(8,128)(2,1)S(1)}, u32[]{:S(2)}, u32[]{:S(2)}) collective-permute-start(bf16[416,128]{1,0:T(8,128)(2,1)S(1)} %get-tuple-element.35.kv_ref.refs_0_), channel_id=1, source_target_pairs={{0,2},{2,0},{4,6},{6,4},{8,10},{10,8},{12,14},{14,12},{16,18},{18,... | collective-permute-start | bytes 319496 | tf_op jit(solution)/shard_map/ppermute | solution.py:385
  6.7 6.8 %collective-permute-start.5 = (bf16[400,128]{1,0:T(8,128)(2,1)S(1)}, bf16[400,128]{1,0:T(8,128)(2,1)S(1)}, u32[]{:S(2)}, u32[]{:S(2)}) collective-permute-start(bf16[400,128]{1,0:T(8,128)(2,1)S(1)} %get-tuple-element.46), channel_id=1, source_target_pairs={{0,16},{2,18},{4,20},{6,22},{8,24},{10,26},{12,28},{14,30},{16,0},... | collective-permute-start | bytes 307208 | tf_op jit(solution)/shard_map/ppermute | solution.py:385
  8.2 2.9 %collective-permute-start.4 = (bf16[384,128]{1,0:T(8,128)(2,1)S(1)}, bf16[384,128]{1,0:T(8,128)(2,1)S(1)}, u32[]{:S(2)}, u32[]{:S(2)}) collective-permute-start(bf16[384,128]{1,0:T(8,128)(2,1)S(1)} %get-tuple-element.38.par_kv_ref.refs_1_), channel_id=1, source_target_pairs={{0,8},{2,4},{4,2},{6,14},{8,0},{10,12},{12,10},{14,6},{16,24},{18,... | collective-permute-start | bytes 294920 | tf_op jit(solution)/shard_map/ppermute | solution.py:385
  8.2 5.2 %collective-permute-start.3 = (bf16[384,128]{1,0:T(8,128)(2,1)S(1)}, bf16[384,128]{1,0:T(8,128)(2,1)S(1)}, u32[]{:S(2)}, u32[]{:S(2)}) collective-permute-start(bf16[384,128]{1,0:T(8,128)(2,1)S(1)} %get-tuple-element.38.par_kv_ref.refs_1_), channel_id=1, source_target_pairs={{0,2},{2,0},{4,6},{6,4},{8,10},{10,8},{12,14},{14,12},{16,18},{18,... | collective-permute-start | bytes 294920 | tf_op jit(solution)/shard_map/ppermute | solution.py:385
  14.1 3.8 %collective-permute-start.6 = (f32[8,384]{1,0:T(8,128)S(1)}, f32[8,384]{1,0:T(8,128)S(1)}, u32[]{:S(2)}, u32[]{:S(2)}) collective-permute-start(f32[8,384]{1,0:T(8,128)S(1)} %get-tuple-element.49.refs_7_.refs_1_), channel_id=1, source_target_pairs={{0,16},{2,18},{4,20},{6,22},{8,24},{10,26},{12,28},{14,30},{16,0},... | collective-permute-start | bytes 36872 | tf_op jit(solution)/shard_map/ppermute | solution.py:385
  18.8 5.7 %collective-permute-start.7 = (bf16[2,384,128]{2,1,0:T(8,128)(2,1)S(1)}, bf16[2,384,128]{2,1,0:T(8,128)(2,1)S(1)}, u32[]{:S(2)}, u32[]{:S(2)}) collective-permute-start(bf16[2,384,128]{2,1,0:T(8,128)(2,1)S(1)} %get-tuple-element.60), channel_id=1, source_target_pairs={{0,2},{2,0},{4,6},{6,4},{8,10},{10,8},{12,14},{14,12},{16,18},{18,... | collective-permute-start | bytes 589832 | tf_op jit(solution)/shard_map/ppermute | solution.py:385
  20.3 4.3 %collective-permute-start.8 = (bf16[2,384,128]{2,1,0:T(8,128)(2,1)S(1)}, bf16[2,384,128]{2,1,0:T(8,128)(2,1)S(1)}, u32[]{:S(2)}, u32[]{:S(2)}) collective-permute-start(bf16[2,384,128]{2,1,0:T(8,128)(2,1)S(1)} %get-tuple-element.61), channel_id=1, source_target_pairs={{0,8},{2,4},{4,2},{6,14},{8,0},{10,12},{12,10},{14,6},{16,24},{18,... | collective-permute-start | bytes 589832 | tf_op jit(solution)/shard_map/ppermute | solution.py:385
  20.3 4.2 %collective-permute-start.9 = (bf16[192,128]{1,0:T(8,128)(2,1)S(1)}, bf16[192,128]{1,0:T(8,128)(2,1)S(1)}, u32[]{:S(2)}, u32[]{:S(2)}) collective-permute-start(bf16[192,128]{1,0:T(8,128)(2,1)S(1)} %get-tuple-element.63), channel_id=1, source_target_pairs={{0,16},{2,18},{4,20},{6,22},{8,24},{10,26},{12,28},{14,30},{16,0},... | collective-permute-start | bytes 147464 | tf_op jit(solution)/shard_map/ppermute | solution.py:385
  24.7 1.4 %collective-permute-start.10 = (bf16[3,192,128]{2,1,0:T(8,128)(2,1)S(1)}, bf16[3,192,128]{2,1,0:T(8,128)(2,1)S(1)}, u32[]{:S(2)}, u32[]{:S(2)}) collective-permute-start(bf16[3,192,128]{2,1,0:T(8,128)(2,1)S(1)} %get-tuple-element.65), channel_id=1, source_target_pairs={{0,8},{8,0},{16,24},{24,16},{1,9},{9,1},{17,25},{25,17},{2,10},{10... | collective-permute-start | bytes 442376 | tf_op jit(solution)/shard_map/ppermute | solution.py:388

commit v4 on v3

--- a/solution.py
+++ b/solution.py
@@ -89,11 +89,11 @@
         ref[pl.ds(2 * tok, 16), :] = jnp.concatenate(lines + [jnp.zeros((1, width), f32)], axis=0).astype(jnp.bfloat16)
 
 
-def foreign_delta(ref, which, tok):
+def foreign_delta(ref, tok):
     terms = ref[pl.ds(2 * tok, 16), :].astype(jnp.float32)
-    one, two = (sum(terms[9 + 2 * i + half : 10 + 2 * i + half] for i in range(3)) for half in range(2))
-    none = jnp.zeros_like(one)
-    return jnp.concatenate([one, two, none] if which == 0 else [none, one, two], axis=1)
+    return jnp.concatenate(
+        [sum(terms[9 + 2 * i + half : 10 + 2 * i + half] for i in range(3)) for half in range(2)], axis=1
+    )
 
 
 def line_place(z, line, heights):
@@ -152,17 +152,19 @@
 
 
 def largest(tok, blocks):
-    top = jnp.full((8, 2 * tok), -1e30, jnp.float32)
+    lanes = blocks[0][0].shape[1]
+    top = jnp.full((8, lanes), -1e30, jnp.float32)
     for ref, i in blocks:
-        top = jnp.maximum(top, jnp.max(ref[rows_at(i, tok), :].reshape(tok // 8, 8, 2 * tok), axis=0))
+        top = jnp.maximum(top, jnp.max(ref[rows_at(i, tok), :].reshape(tok // 8, 8, lanes), axis=0))
     return jnp.max(top, axis=0, keepdims=True)
 
 
 def summed(tok, blocks, top):
-    total = jnp.zeros((8, 2 * tok), jnp.float32)
+    lanes = blocks[0][0].shape[1]
+    total = jnp.zeros((8, lanes), jnp.float32)
     for ref, i in blocks:
         weights = jnp.exp(ref[rows_at(i, tok), :] - top)
-        total = total + jnp.sum(weights.reshape(tok // 8, 8, 2 * tok), axis=0)
+        total = total + jnp.sum(weights.reshape(tok // 8, 8, lanes), axis=0)
     return jnp.sum(total, axis=0, keepdims=True)
 
 
@@ -179,7 +181,17 @@
 
 def foreign_rows(ref, part, which, tok):
     block = ref[rows_at(part, tok), :]
-    return jnp.concatenate([block, jnp.zeros_like(block)] if which == 0 else [jnp.zeros_like(block), block], axis=0)
+    gap = jnp.zeros((2 * block.shape[1] - tok, block.shape[1]), block.dtype)
+    return jnp.concatenate([block, gap] if which == 0 else [gap, block], axis=0)
+
+
+def foreign_lanes(which, tok, width):
+    return slice(0, 2 * width) if which == 0 else slice(2 * tok - 2 * width, 2 * tok)
+
+
+def to_lanes(which, tok, row, fill):
+    gap = jnp.full((1, 2 * tok - row.shape[1]), fill, jnp.float32)
+    return jnp.concatenate([row, gap] if which == 0 else [gap, row], axis=1)
 
 
 def score_kernel(tok, chips, heights, sides, scale, qg, table, part, *refs):
@@ -197,14 +209,21 @@
         for line in range(3):
             inside, at = line_place(z, line, heights)
             row = jnp.where(rising, at(flags, 0), at(flags, 2))
-            none = jnp.zeros_like(row)
-            row = lanes_of(tok, *((row, none) if which == 0 else (none, row)))
+            lane = lax.broadcasted_iota(jnp.int32, row.shape, 1)
+            width = row.shape[1]
+            row = jnp.concatenate(
+                [
+                    jnp.where(lane + start < tok if which == 0 else lane + start >= 2 * width - tok, row, 0.0)
+                    for start in (0, width)
+                ],
+                axis=1,
+            )
             bias = jnp.where(inside & within(y_at, chips), (row - 1.0) * 1e30, -1e30)
             border = pick(near, which, keys[2 * line][rows_at(0, tok), :], keys[2 * line + 1][rows_at(0, tok), :])
             s_far[rows_at(3 * which + line, tok), :] = dot(border, queries, ROWS_T) * scale + bias
         blocks = [(s_far, 3 * which + line) for line in range(3)]
         top = largest(tok, blocks)
-        far.append([top, summed(tok, blocks, top)])
+        far.append([to_lanes(which, tok, top, -1e30), to_lanes(which, tok, summed(tok, blocks, top), 0.0)])
     for i in range(2):
         scores = dot(keys[3 + 2 * i][rows_at(0, tok), :], qg[0], ROWS_T) * scale
         s_late[rows_at(i, tok), :] = scores + table[3 + 2 * i : 4 + 2 * i, :]
@@ -237,13 +256,14 @@
     dq_ref[...] = dq
     for which in range(sides):
         far_g = foreign_rows(foreign[which], 1, which, tok)
-        delta = foreign_delta(foreign[which], which, tok)
-        dq = jnp.zeros(dq_ref.shape, f32)
+        delta = foreign_delta(foreign[which], tok)
+        lanes = foreign_lanes(which, tok, qg.shape[2])
+        dq = jnp.zeros(far_dq[which].shape, f32)
         for line in range(3):
             rows = rows_at(3 * which + line, tok)
             own, par = tiles[2 * line], tiles[2 * line + 1]
             key, value = (pick(near, which, own[rows_at(i, tok), :], par[rows_at(i, tok), :]) for i in range(2))
-            weights = jnp.exp(s_far[rows, :] - sent[which][2:3, :])
+            weights = jnp.exp(s_far[rows, :] - sent[which][2:3, lanes])
             low = (weights * (dot(value, far_g, ROWS_T) - delta) * scale).astype(bf16)
             e_far[rows, :] = weights.astype(bf16)
             ds_far[rows, :] = low
@@ -251,15 +271,17 @@
         far_dq[which][...] = dq
 
 
-def column_sums(tok, near, sides, line, slot, e_ref, ds_ref, e_far, ds_far, scaled, far_scaled):
-    rows = rows_at(2 * line + slot, tok)
-    sums = [dot(ds_ref[rows, :], scaled[0]), dot(e_ref[rows, :], scaled[1])]
+def column_sums(tok, near, sides, line, e_ref, ds_ref, e_far, ds_far, scaled, far_scaled):
+    rows = [rows_at(2 * line + slot, tok) for slot in range(2)]
+    sums = [[dot(ref[at, :], scaled[i]) for i, ref in enumerate((ds_ref, e_ref))] for at in rows]
     for which in range(sides):
-        rows = rows_at(3 * which + line, tok)
-        mine = near == ((slot == 0) == (which == 0))
+        at = rows_at(3 * which + line, tok)
         for i, ref in enumerate((ds_far, e_far)):
-            sums[i] = sums[i] + jnp.where(mine, dot(ref[rows, :], far_scaled[which][i]), 0.0)
-    return [part.astype(jnp.bfloat16) for part in sums]
+            far = dot(ref[at, :], far_scaled[which][i])
+            for slot in range(2):
+                mine = near == ((slot == 0) == (which == 0))
+                sums[slot][i] = sums[slot][i] + jnp.where(mine, far, 0.0)
+    return [[part.astype(jnp.bfloat16) for part in pair] for pair in sums]
 
 
 def leave_kernel(tok, chips, sides, qg, e_ref, ds_ref, e_far, ds_far, *refs):
@@ -276,7 +298,7 @@
         return both + jnp.log(total * jnp.exp(top - both) + other_total * jnp.exp(other_top - both))
 
     def times(block, factor):
-        return (block.astype(jnp.float32) * jnp.broadcast_to(factor, (width, 2 * tok)).T).astype(bf16)
+        return (block.astype(jnp.float32) * jnp.broadcast_to(factor, (width, factor.shape[1])).T).astype(bf16)
 
     top, total = sent[0][0:1, :], sent[0][1:2, :]
     lse = None
@@ -285,9 +307,10 @@
         inside = within(y_at, chips)
         note = came[which]
         far_lse = log_total(note[0:1, :], note[1:2, :], sent[which][2:3, :], sent[which][3:4, :])
-        factor = jnp.where(inside, jnp.exp(sent[which][2:3, :] - far_lse), 0.0)
+        lanes = foreign_lanes(which, tok, width)
+        factor = jnp.where(inside, jnp.exp(sent[which][2:3, lanes] - far_lse[:, lanes]), 0.0)
         share = (far_dq[which][...] * factor).T
-        shares[which][...] = share[which * tok : (which + 1) * tok].astype(bf16)
+        shares[which][...] = (share[:tok] if which == 0 else share[2 * width - tok :]).astype(bf16)
         for part in range(2):
             far_scaled[which][part] = times(foreign_rows(foreign[which], part, which, tok), factor)
         other = jnp.where(inside, note[2:3, :], -1e30), jnp.where(inside, note[3:4, :], 0.0)
@@ -297,20 +320,20 @@
     for part in range(2):
         scaled[part] = times(qg[part], factor)
     for line, result in ((1, one_ref), (2, two_ref)):
+        sums = column_sums(tok, near, sides, line, e_ref, ds_ref, e_far, ds_far, scaled, far_scaled)
         for slot in range(2):
-            sums = column_sums(tok, near, sides, line, slot, e_ref, ds_ref, e_far, ds_far, scaled, far_scaled)
             for i in range(2):
-                result[i, rows_at(slot, tok), :] = sums[i]
+                result[i, rows_at(slot, tok), :] = sums[slot][i]
 
 
 def stay_kernel(tok, sides, e_ref, ds_ref, e_far, ds_far, scaled, factor_ref, raw_dq, *refs):
     far_scaled, (own_ref, dq_ref) = refs[:sides], refs[sides:]
     y, c, _ = place()
     near = border_is_own(y, c)
+    sums = column_sums(tok, near, sides, 0, e_ref, ds_ref, e_far, ds_far, scaled, far_scaled)
     for slot in range(2):
-        sums = column_sums(tok, near, sides, 0, slot, e_ref, ds_ref, e_far, ds_far, scaled, far_scaled)
         for i in range(2):
-            own_ref[i, rows_at(slot, tok), :] = sums[i]
+            own_ref[i, rows_at(slot, tok), :] = sums[slot][i]
     dq_ref[...] = (raw_dq[...] * factor_ref[0:1, :]).T
 
 
@@ -388,7 +411,7 @@
         return lax.ppermute(block, "tm", [(t, t ^ 1) for t in range(times)])
 
     line_shape, tile_shape = ((2, 2 * tok, width), bf16), ((2, tok, width), bf16)
-    extra = 32
+    extra = 48
     arguments = (keys, values, queries, grad_out, attn_out, window_mask)
     kv, rest, other = call(
         functools.partial(pack_kernel, tok),
@@ -400,7 +423,7 @@
     par = swap_cores(other)
     border_shape, two = ((2 * tok + 16, width), bf16), 2 * tok
     par_kv, *borders = call(
-        functools.partial(line_kernel, tok), [((2 * tok, width), bf16)] + [border_shape] * sides, [VMEM] * 2
+        functools.partial(line_kernel, tok), [((2 * tok + 32, width), bf16)] + [border_shape] * sides, [VMEM] * 2
     )(rest, par)
     foreign = [exchange(borders[which], which, None) for which in range(sides)]
     late = [exchange(par_kv, None, which) for which in range(2)]
@@ -409,6 +432,9 @@
 
     def square(count, kind=f32):
         return ((count * tok, two), kind)
+
+    def far_square(kind=f32):
+        return ((3 * sides * tok, 2 * width), kind)
 
     qg, table, s_own, d_own = call(
         functools.partial(first_kernel, tok, heights, scale),
@@ -420,18 +446,18 @@
     )(qg, table, s_own, *early)
     s_late, s_far, *sent = call(
         functools.partial(score_kernel, tok, chips, heights, sides, scale),
-        [square(2), square(3 * sides)] + [note_shape] * sides,
+        [square(2), far_square()] + [note_shape] * sides,
         [VMEM] * (9 + sides),
     )(qg, table, part, *tiles, *foreign)
     came = [exchange(sent[which], which, None) for which in range(sides)]
     e, ds, e_far, ds_far, raw_dq, *far_dq = call(
         functools.partial(middle_kernel, tok, sides, scale),
-        [square(6, bf16)] * 2 + [square(3 * sides, bf16)] * 2 + [raw_shape] * (1 + sides),
+        [square(6, bf16)] * 2 + [far_square(bf16)] * 2 + [raw_shape] + [((width, 2 * width), f32)] * sides,
         [VMEM] * (14 + 2 * sides),
     )(qg, table, s_own, d_own, s_early, d_early, s_late, s_far, *tiles, *foreign, *sent)
     one, other_one, scaled, factor, *rest_out = call(
         functools.partial(leave_kernel, tok, chips, sides),
-        [line_shape, line_shape, pair_shape, note_shape] + [((tok, width), bf16)] * sides + [pair_shape] * sides,
+        [line_shape, line_shape, pair_shape, note_shape] + [((tok, width), bf16)] * sides + [((2, 2 * width, width), bf16)] * sides,
         [VMEM] * (5 + 4 * sides),
     )(qg, e, ds, e_far, ds_far, *far_dq, *sent, *came, *foreign)
     shares, far_scaled = rest_out[:sides], rest_out[sides:]

time: 27 us -> 26.7 us (0.989)
  starting transfers between devices: 11 us -> 12.1 us
  waiting for transfers between devices: 8.78 us -> 7.87 us
  Pallas kernels: 6.38 us -> 5.88 us
    ppermute x9, starting transfers between devices: 10.4 us -> 11.5 us  [exchange(): return lax.ppermute(block, ('tm', 'height'), pairs)]
    ppermute x9, waiting for transfers between devices: 7.42 us -> 6.51 us  [exchange(): return lax.ppermute(block, ('tm', 'height'), pairs)]
where the time goes in v4:
time: 26.7 us; the launch traced here: 26.6 us
  starting transfers between devices  12.1 us (45%)
  waiting for transfers between devices  7.87 us (29%)
  Pallas kernels  5.88 us (22%)
  between operations  0.73 us (3%)
    ppermute x9, starting transfers between devices, exchange(): return lax.ppermute(block, ('tm', 'height'), pairs)  11.5 us
    ppermute x9, waiting for transfers between devices, exchange(): return lax.ppermute(block, ('tm', 'height'), pairs)  6.51 us
    ppermute x2, waiting for transfers between devices, swap_cores(): return lax.ppermute(block, 'tm', [(t, t ^ 1) for t in range(times)])  1.36 us
    pallas_call x1, Pallas kernels, body(): call(functools.partial(middle_kernel, tok, sides, scale), [square(6, bf16...  1.2 us
    pallas_call x1, Pallas kernels, body(): call(functools.partial(pack_kernel, tok), [((2 * tok + extra, width), bf1...  1.12 us
    pallas_call x1, Pallas kernels, body(): call(functools.partial(leave_kernel, tok, chips, sides), [line_shape, lin...  0.77 us
    pallas_call x1, Pallas kernels, body(): call(final_kernel, [(queries.shape, bf16)] * 3, [VMEM] * 3)  0.74 us
    ppermute x2, starting transfers between devices, swap_cores(): return lax.ppermute(block, 'tm', [(t, t ^ 1) for t in range(times)])  0.59 us
  transfers between devices with their start and end apart: 11, of which 5 were waited for; matrix products, arithmetic and copies ran while one was open for 0% of the time, Pallas kernels for 10%

profile of v4, /device:TPU:0, one launch (start us, length us, event | category | flops | bytes accessed | tf_op | source)
XLA Modules:
  0.0 26.6 jit_solution(8887210548277266389)
XLA Ops:
  0.6 1.1 %shard_map.85 = (bf16[432,128]{1,0:T(8,128)(2,1)S(1)}, bf16[592,128]{1,0:T(8,128)(2,1)S(1)}, bf16[976,128]{1,0:T(8,128)(2,1)S(1)}) custom-call(bf16[1,1,2,1,192,128]{5,4,3,2,1,0:T(8,128)(2,1)} %k_ref.1, bf16[1,1,2,1,192,128]{5,4,3,2,1,0:T(8,128)(2,1)} %v_ref.1, bf16[1,1,2,1,192,128]{5,4,3,2,1,0:T(8,128)(2,1)} %q_ref.1, ...), custom_call_target="tpu_custom_call" | custom-call | tf_op jit(solution)/shard_map/pallas_call | solution.py:416
  1.8 0.5 %collective-permute-start = (bf16[976,128]{1,0:T(8,128)(2,1)S(1)}, bf16[976,128]{1,0:T(8,128)(2,1)S(1)}, u32[]{:S(2)}, u32[]{:S(2)}) collective-permute-start(bf16[976,128]{1,0:T(8,128)(2,1)S(1)} %get-tuple-element.37), channel_id=1, source_target_pairs={{0,8},{8,0},{16,24},{24,16},{1,9},{9,1},{17,25},{25,17},{2,10},{10... | collective-permute-start | bytes 749576 | tf_op jit(solution)/shard_map/ppermute | solution.py:411
  2.3 0.1 collective-permute-start.2
  2.4 4.1 %collective-permute-start.1 = (bf16[432,128]{1,0:T(8,128)(2,1)S(1)}, bf16[432,128]{1,0:T(8,128)(2,1)S(1)}, u32[]{:S(2)}, u32[]{:S(2)}) collective-permute-start(bf16[432,128]{1,0:T(8,128)(2,1)S(1)} %get-tuple-element.35.kv_ref.refs_0_), channel_id=1, source_target_pairs={{0,2},{2,0},{4,6},{6,4},{8,10},{10,8},{12,14},{14,12},{16,18},{18,... | collective-permute-start | bytes 331784 | tf_op jit(solution)/shard_map/ppermute | solution.py:408
  6.5 0.1 shard_map.86
  6.7 0.1 collective-permute-start.4
  6.7 2.0 %collective-permute-start.3 = (bf16[416,128]{1,0:T(8,128)(2,1)S(1)}, bf16[416,128]{1,0:T(8,128)(2,1)S(1)}, u32[]{:S(2)}, u32[]{:S(2)}) collective-permute-start(bf16[416,128]{1,0:T(8,128)(2,1)S(1)} %get-tuple-element.38.par_kv_ref.refs_1_), channel_id=1, source_target_pairs={{0,2},{2,0},{4,6},{6,4},{8,10},{10,8},{12,14},{14,12},{16,18},{18,... | collective-permute-start | bytes 319496 | tf_op jit(solution)/shard_map/ppermute | solution.py:408
  8.7 1.5 %collective-permute-start.5 = (bf16[400,128]{1,0:T(8,128)(2,1)S(1)}, bf16[400,128]{1,0:T(8,128)(2,1)S(1)}, u32[]{:S(2)}, u32[]{:S(2)}) collective-permute-start(bf16[400,128]{1,0:T(8,128)(2,1)S(1)} %get-tuple-element.46), channel_id=1, source_target_pairs={{0,16},{2,18},{4,20},{6,22},{8,24},{10,26},{12,28},{14,30},{16,0},... | collective-permute-start | bytes 307208 | tf_op jit(solution)/shard_map/ppermute | solution.py:408
  10.3 0.4 %shard_map.87 = (bf16[2,384,128]{2,1,0:T(8,128)(2,1)S(1)}, f32[8,384]{1,0:T(8,128)S(1)}, f32[384,384]{1,0:T(8,128)S(1)}, f32[384,384]{1,0:T(8,128)S(1)}) custom-call(bf16[432,128]{1,0:T(8,128)(2,1)S(1)} %get-tuple-element.35.kv_ref.refs_0_, bf16[416,128]{1,0:T(8,128)(2,1)S(1)} %get-tuple-element.38.par_kv_ref.refs_1_, ...), custom_call_target="tpu_custom_call" | custom-call | tf_op jit(solution)/shard_map/pallas_call | solution.py:439
  10.7 0.5 %shard_map.88 = (f32[384,384]{1,0:T(8,128)S(1)}, f32[384,384]{1,0:T(8,128)S(1)}, f32[8,384]{1,0:T(8,128)S(1)}) custom-call(bf16[2,384,128]{2,1,0:T(8,128)(2,1)S(1)} %get-tuple-element.39.qg, f32[8,384]{1,0:T(8,128)S(1)} %get-tuple-element.40.table, f32[384,384]{1,0:T(8,128)S(1)} %get-tuple-element.41.s_own, ...), custom_call_target="tpu_custom_call" | custom-call | tf_op jit(solution)/shard_map/pallas_call | solution.py:444
  11.2 2.2 %collective-permute-done.5.refs_6_.refs_3_ = bf16[400,128]{1,0:T(8,128)(2,1)S(1)} collective-permute-done((bf16[400,128]{1,0:T(8,128)(2,1)S(1)}, bf16[400,128]{1,0:T(8,128)(2,1)S(1)}, u32[]{:S(2)}, u32[]{:S(2)}) %collective-permute-start.5) | collective-permute-done | bytes 102432 | tf_op jit(solution)/shard_map/ppermute | solution.py:408
  13.4 0.5 %shard_map.89 = (f32[384,384]{1,0:T(8,128)S(1)}, f32[576,256]{1,0:T(8,128)S(1)}, f32[8,384]{1,0:T(8,128)S(1)}) custom-call(bf16[2,384,128]{2,1,0:T(8,128)(2,1)S(1)} %get-tuple-element.39.qg, f32[8,384]{1,0:T(8,128)S(1)} %get-tuple-element.40.table, f32[8,384]{1,0:T(8,128)S(1)} %get-tuple-element.45.part, ...), custom_call_target="tpu_custom_call" | custom-call | tf_op jit(solution)/shard_map/pallas_call | solution.py:447
  14.0 1.6 %collective-permute-start.6 = (f32[8,384]{1,0:T(8,128)S(1)}, f32[8,384]{1,0:T(8,128)S(1)}, u32[]{:S(2)}, u32[]{:S(2)}) collective-permute-start(f32[8,384]{1,0:T(8,128)S(1)} %get-tuple-element.49.refs_7_.refs_1_), channel_id=1, source_target_pairs={{0,16},{2,18},{4,20},{6,22},{8,24},{10,26},{12,28},{14,30},{16,0},... | collective-permute-start | bytes 36872 | tf_op jit(solution)/shard_map/ppermute | solution.py:408
  15.5 1.2 %shard_map.90 = (bf16[1152,384]{1,0:T(8,128)(2,1)S(1)}, bf16[1152,384]{1,0:T(8,128)(2,1)S(1)}, bf16[576,256]{1,0:T(8,128)(2,1)S(1)}, bf16[576,256]{1,0:T(8,128)(...) custom-call(bf16[2,384,128]{2,1,0:T(8,128)(2,1)S(1)} %get-tuple-element.39.qg, ...), custom_call_target="tpu_custom_call" | custom-call | tf_op jit(solution)/shard_map/pallas_call | solution.py:453
  16.7 1.0 %collective-permute-done.6.refs_2_ = f32[8,384]{1,0:T(8,128)S(1)} collective-permute-done((f32[8,384]{1,0:T(8,128)S(1)}, f32[8,384]{1,0:T(8,128)S(1)}, u32[]{:S(2)}, u32[]{:S(2)}) %collective-permute-start.6) | collective-permute-done | bytes 12320 | tf_op jit(solution)/shard_map/ppermute | solution.py:408
  17.7 0.8 %shard_map.91 = (bf16[2,384,128]{2,1,0:T(8,128)(2,1)S(1)}, bf16[2,384,128]{2,1,0:T(8,128)(2,1)S(1)}, bf16[2,384,128]{2,1,0:T(8,128)(2,1)S(1)}, f32[8,384]{1,0:T(...) custom-call(bf16[2,384,128]{2,1,0:T(8,128)(2,1)S(1)} %get-tuple-element.39.qg, ...), custom_call_target="tpu_custom_call" | custom-call | tf_op jit(solution)/shard_map/pallas_call | solution.py:458
  18.5 0.6 %collective-permute-start.7 = (bf16[2,384,128]{2,1,0:T(8,128)(2,1)S(1)}, bf16[2,384,128]{2,1,0:T(8,128)(2,1)S(1)}, u32[]{:S(2)}, u32[]{:S(2)}) collective-permute-start(bf16[2,384,128]{2,1,0:T(8,128)(2,1)S(1)} %get-tuple-element.60), channel_id=1, source_target_pairs={{0,2},{2,0},{4,6},{6,4},{8,10},{10,8},{12,14},{14,12},{16,18},{18,... | collective-permute-start | bytes 589832 | tf_op jit(solution)/shard_map/ppermute | solution.py:408
  19.1 1.5 %collective-permute-start.9 = (bf16[192,128]{1,0:T(8,128)(2,1)S(1)}, bf16[192,128]{1,0:T(8,128)(2,1)S(1)}, u32[]{:S(2)}, u32[]{:S(2)}) collective-permute-start(bf16[192,128]{1,0:T(8,128)(2,1)S(1)} %get-tuple-element.63), channel_id=1, source_target_pairs={{0,16},{2,18},{4,20},{6,22},{8,24},{10,26},{12,28},{14,30},{16,0},... | collective-permute-start | bytes 147464 | tf_op jit(solution)/shard_map/ppermute | solution.py:408
  20.6 0.4 %shard_map.92 = (bf16[2,384,128]{2,1,0:T(8,128)(2,1)S(1)}, f32[384,128]{1,0:T(8,128)S(1)}) custom-call(bf16[1152,384]{1,0:T(8,128)(2,1)S(1)} %get-tuple-element.50.e_ref, bf16[1152,384]{1,0:T(8,128)(2,1)S(1)} %get-tuple-element.51.ds_ref, bf16[576,256]{1,0:T(8,128)(2,1)S(1)} %get-tuple-element.52.e_far, bf16[576,256]{1,0:T(8,128)(2,1)S(1)} %get-tuple-element.53.ds_far, ...), custom_call_target="tpu_custom_call" | custom-call | tf_op jit(solution)/shard_map/pallas_call | solution.py:466
  21.0 2.3 %collective-permute-done.9.refs_0_ = bf16[192,128]{1,0:T(8,128)(2,1)S(1)} collective-permute-done((bf16[192,128]{1,0:T(8,128)(2,1)S(1)}, bf16[192,128]{1,0:T(8,128)(2,1)S(1)}, u32[]{:S(2)}, u32[]{:S(2)}) %collective-permute-start.9) | collective-permute-done | bytes 49184 | tf_op jit(solution)/shard_map/ppermute | solution.py:408
  23.2 1.0 %collective-permute-done.7.one_ref = bf16[2,384,128]{2,1,0:T(8,128)(2,1)S(1)} collective-permute-done((bf16[2,384,128]{2,1,0:T(8,128)(2,1)S(1)}, bf16[2,384,128]{2,1,0:T(8,128)(2,1)S(1)}, u32[]{:S(2)}, u32[]{:S(2)}) %collective-permute-start.7) | collective-permute-done | bytes 196640 | tf_op jit(solution)/shard_map/ppermute | solution.py:408
  24.2 0.1 shard_map.93
  24.5 1.4 %collective-permute-done.10.swap_ref = bf16[3,192,128]{2,1,0:T(8,128)(2,1)S(1)} collective-permute-done((bf16[3,192,128]{2,1,0:T(8,128)(2,1)S(1)}, bf16[3,192,128]{2,1,0:T(8,128)(2,1)S(1)}, u32[]{:S(2)}, u32[]{:S(2)}) %collective-permute-start.10) | collective-permute-done | bytes 147488 | tf_op jit(solution)/shard_map/ppermute | solution.py:411
  25.8 0.7 %shard_map.94 = (bf16[1,1,2,1,192,128]{5,4,3,2,1,0:T(8,128)(2,1)}, bf16[1,1,2,1,192,128]{5,4,3,2,1,0:T(8,128)(2,1)}, bf16[1,1,2,1,192,128]{5,4,3,2,1,0:T(8,128)(2,1)}) custom-call(bf16[2,192,128]{2,1,0:T(8,128)(2,1)S(1)} %get-tuple-element.64.mine_ref, bf16[3,192,128]{2,1,0:T(8,128)(2,1)S(1)} %collective-permute-done.10.swap_ref, ...), custom_call_target="tpu_custom_call" | custom-call | tf_op jit(solution)/shard_map/pallas_call | solution.py:476
  (8 shorter events, 0.1 us)
Async XLA Ops:
  1.8 4.7 %collective-permute-start = (bf16[976,128]{1,0:T(8,128)(2,1)S(1)}, bf16[976,128]{1,0:T(8,128)(2,1)S(1)}, u32[]{:S(2)}, u32[]{:S(2)}) collective-permute-start(bf16[976,128]{1,0:T(8,128)(2,1)S(1)} %get-tuple-element.37), channel_id=1, source_target_pairs={{0,8},{8,0},{16,24},{24,16},{1,9},{9,1},{17,25},{25,17},{2,10},{10... | collective-permute-start | bytes 749576 | tf_op jit(solution)/shard_map/ppermute | solution.py:411
  2.3 8.4 %collective-permute-start.2 = (bf16[432,128]{1,0:T(8,128)(2,1)S(1)}, bf16[432,128]{1,0:T(8,128)(2,1)S(1)}, u32[]{:S(2)}, u32[]{:S(2)}) collective-permute-start(bf16[432,128]{1,0:T(8,128)(2,1)S(1)} %get-tuple-element.35.kv_ref.refs_0_), channel_id=1, source_target_pairs={{0,8},{2,4},{4,2},{6,14},{8,0},{10,12},{12,10},{14,6},{16,24},{18,... | collective-permute-start | bytes 331784 | tf_op jit(solution)/shard_map/ppermute | solution.py:408
  2.4 8.3 %collective-permute-start.1 = (bf16[432,128]{1,0:T(8,128)(2,1)S(1)}, bf16[432,128]{1,0:T(8,128)(2,1)S(1)}, u32[]{:S(2)}, u32[]{:S(2)}) collective-permute-start(bf16[432,128]{1,0:T(8,128)(2,1)S(1)} %get-tuple-element.35.kv_ref.refs_0_), channel_id=1, source_target_pairs={{0,2},{2,0},{4,6},{6,4},{8,10},{10,8},{12,14},{14,12},{16,18},{18,... | collective-permute-start | bytes 331784 | tf_op jit(solution)/shard_map/ppermute | solution.py:408
  6.7 6.7 %collective-permute-start.4 = (bf16[416,128]{1,0:T(8,128)(2,1)S(1)}, bf16[416,128]{1,0:T(8,128)(2,1)S(1)}, u32[]{:S(2)}, u32[]{:S(2)}) collective-permute-start(bf16[416,128]{1,0:T(8,128)(2,1)S(1)} %get-tuple-element.38.par_kv_ref.refs_1_), channel_id=1, source_target_pairs={{0,8},{2,4},{4,2},{6,14},{8,0},{10,12},{12,10},{14,6},{16,24},{18,... | collective-permute-start | bytes 319496 | tf_op jit(solution)/shard_map/ppermute | solution.py:408
  6.7 6.7 %collective-permute-start.3 = (bf16[416,128]{1,0:T(8,128)(2,1)S(1)}, bf16[416,128]{1,0:T(8,128)(2,1)S(1)}, u32[]{:S(2)}, u32[]{:S(2)}) collective-permute-start(bf16[416,128]{1,0:T(8,128)(2,1)S(1)} %get-tuple-element.38.par_kv_ref.refs_1_), channel_id=1, source_target_pairs={{0,2},{2,0},{4,6},{6,4},{8,10},{10,8},{12,14},{14,12},{16,18},{18,... | collective-permute-start | bytes 319496 | tf_op jit(solution)/shard_map/ppermute | solution.py:408
  8.7 4.7 %collective-permute-start.5 = (bf16[400,128]{1,0:T(8,128)(2,1)S(1)}, bf16[400,128]{1,0:T(8,128)(2,1)S(1)}, u32[]{:S(2)}, u32[]{:S(2)}) collective-permute-start(bf16[400,128]{1,0:T(8,128)(2,1)S(1)} %get-tuple-element.46), channel_id=1, source_target_pairs={{0,16},{2,18},{4,20},{6,22},{8,24},{10,26},{12,28},{14,30},{16,0},... | collective-permute-start | bytes 307208 | tf_op jit(solution)/shard_map/ppermute | solution.py:408
  14.0 3.8 %collective-permute-start.6 = (f32[8,384]{1,0:T(8,128)S(1)}, f32[8,384]{1,0:T(8,128)S(1)}, u32[]{:S(2)}, u32[]{:S(2)}) collective-permute-start(f32[8,384]{1,0:T(8,128)S(1)} %get-tuple-element.49.refs_7_.refs_1_), channel_id=1, source_target_pairs={{0,16},{2,18},{4,20},{6,22},{8,24},{10,26},{12,28},{14,30},{16,0},... | collective-permute-start | bytes 36872 | tf_op jit(solution)/shard_map/ppermute | solution.py:408
  18.5 5.7 %collective-permute-start.7 = (bf16[2,384,128]{2,1,0:T(8,128)(2,1)S(1)}, bf16[2,384,128]{2,1,0:T(8,128)(2,1)S(1)}, u32[]{:S(2)}, u32[]{:S(2)}) collective-permute-start(bf16[2,384,128]{2,1,0:T(8,128)(2,1)S(1)} %get-tuple-element.60), channel_id=1, source_target_pairs={{0,2},{2,0},{4,6},{6,4},{8,10},{10,8},{12,14},{14,12},{16,18},{18,... | collective-permute-start | bytes 589832 | tf_op jit(solution)/shard_map/ppermute | solution.py:408
  19.1 5.2 %collective-permute-start.8 = (bf16[2,384,128]{2,1,0:T(8,128)(2,1)S(1)}, bf16[2,384,128]{2,1,0:T(8,128)(2,1)S(1)}, u32[]{:S(2)}, u32[]{:S(2)}) collective-permute-start(bf16[2,384,128]{2,1,0:T(8,128)(2,1)S(1)} %get-tuple-element.61), channel_id=1, source_target_pairs={{0,8},{2,4},{4,2},{6,14},{8,0},{10,12},{12,10},{14,6},{16,24},{18,... | collective-permute-start | bytes 589832 | tf_op jit(solution)/shard_map/ppermute | solution.py:408
  19.1 4.2 %collective-permute-start.9 = (bf16[192,128]{1,0:T(8,128)(2,1)S(1)}, bf16[192,128]{1,0:T(8,128)(2,1)S(1)}, u32[]{:S(2)}, u32[]{:S(2)}) collective-permute-start(bf16[192,128]{1,0:T(8,128)(2,1)S(1)} %get-tuple-element.63), channel_id=1, source_target_pairs={{0,16},{2,18},{4,20},{6,22},{8,24},{10,26},{12,28},{14,30},{16,0},... | collective-permute-start | bytes 147464 | tf_op jit(solution)/shard_map/ppermute | solution.py:408
  24.4 1.4 %collective-permute-start.10 = (bf16[3,192,128]{2,1,0:T(8,128)(2,1)S(1)}, bf16[3,192,128]{2,1,0:T(8,128)(2,1)S(1)}, u32[]{:S(2)}, u32[]{:S(2)}) collective-permute-start(bf16[3,192,128]{2,1,0:T(8,128)(2,1)S(1)} %get-tuple-element.65), channel_id=1, source_target_pairs={{0,8},{8,0},{16,24},{24,16},{1,9},{9,1},{17,25},{25,17},{2,10},{10... | collective-permute-start | bytes 442376 | tf_op jit(solution)/shard_map/ppermute | solution.py:411
